TPU v7x, 32 devices: a whole 2x2x4 slice. The times are simulated.
32 devices in a mesh: seq: 8 (over z, y), mp: 4 (over x, core).
Axes of the slice: x: 2, y: 2, z: 4, core: 2. Of those that a mesh axis runs over, the one named last changes fastest.
Arguments:
- mixed_in: bfloat16 [4096, 2048], P('seq'), may hold values from -6 to 6
- w_query: bfloat16 [2048, 2048], P(None, 'mp'), may hold values from -0.1875 to 0.1875
- w_key: bfloat16 [2048, 2048], P(None, 'mp'), may hold values from -0.1875 to 0.1875
- w_value: bfloat16 [2048, 2048], P(None, 'mp'), may hold values from -0.125 to 0.125
- w_out: bfloat16 [2048, 2048], P('mp'), may hold values from -0.375 to 0.375
- gain_attn: float32 [2048], replicated, may hold values from 0.1 to 1.9
- w_gate: bfloat16 [2048, 8192], P(None, 'mp'), may hold values from -0.125 to 0.125
- w_up: bfloat16 [2048, 8192], P(None, 'mp'), may hold values from -0.125 to 0.125
- w_down: bfloat16 [8192, 2048], P('mp'), may hold values from -0.125 to 0.125
- gain_mlp: float32 [2048], replicated, may hold values from 0.1 to 1.9
- doc_ends: int32 [5], replicated, may hold values from 1 to 4096, as said below
- cotangent: bfloat16 [4096, 2048], P('seq'), may hold values from -6 to 6
Outputs:
- mixed_out: bfloat16 [4096, 2048], P('seq')
- input_grad: bfloat16 [4096, 2048], P('seq')
- grad_query: float32 [2048, 2048], P('seq', 'mp')
- grad_key: float32 [2048, 2048], P('seq', 'mp')
- grad_value: float32 [2048, 2048], P('seq', 'mp')
- grad_out: float32 [2048, 2048], P('mp', 'seq')
- grad_gain_attn: float32 [2048], P('seq')
- grad_gate: float32 [2048, 8192], P('seq', 'mp')
- grad_up: float32 [2048, 8192], P('seq', 'mp')
- grad_down: float32 [8192, 2048], P('mp', 'seq')
- grad_gain_mlp: float32 [2048], P('seq')
Inputs may be any that keep to these rules, and one draw needn't show every extreme that they name: `doc_ends`: rising ends of the 5 packed documents; the last is 4096; one document begins within the first 512 tokens and ends within the last 512 tokens; each of the others holds 1 to 128 tokens.
All inputs are finite; a program needn't handle non-finite values.
Results may differ from a plain program's by a relative error of at most 0.017.
Values may be sent and summed in bfloat16 or wider, within the bound.
No kernel may reach another device: no remote copies, remote signals or barrier semaphores. Data moves between devices by JAX's collectives and lax.ppermute only.
A program may use at most 256 MiB of HBM per device.

v0:
```python
import functools
import math
import types

import jax
import jax.numpy as jnp
from jax import lax
from jax.experimental import pallas as pl
from jax.experimental.pallas import tpu as pltpu
from jax.sharding import PartitionSpec as P

HD = 128
EPSILON = 1e-05
THETA = 10000.0
FACTOR = 1.0 / math.sqrt(HD)
CLAMP = 80.0
CHUNKS = 2
SHARE = 0.5
ORDER = []
MIB = 1024 * 1024
F32 = jnp.float32
BF16 = jnp.bfloat16


def nn(left, right):
    return lax.dot_general(left, right, (((1,), (0,)), ((), ())), preferred_element_type=F32)


def nt(left, right):
    return lax.dot_general(left, right, (((1,), (1,)), ((), ())), preferred_element_type=F32)


def tn(left, right):
    return lax.dot_general(left, right, (((0,), (0,)), ((), ())), preferred_element_type=F32)


def call(
    body,
    out_shape,
    operands,
    in_specs,
    flops,
    moved,
    transcendentals=0,
    after=(),
    prefetch=0,
    chain=True,
    vmem=20,
    **kwargs,
):
    n = prefetch + len(in_specs)
    after = list(after) + (ORDER if chain else [])

    def kernel(*refs):
        body(*refs[:n], *refs[n + len(after) :])

    in_specs = list(in_specs) + [pl.BlockSpec(memory_space=pl.ANY)] * len(after)
    if prefetch:
        kwargs = {
            "name": kwargs.pop("name"),
            "grid_spec": pltpu.PrefetchScalarGridSpec(
                num_scalar_prefetch=prefetch, in_specs=in_specs, **kwargs
            ),
        }
    else:
        kwargs["in_specs"] = in_specs
    made = pl.pallas_call(
        kernel,
        out_shape=out_shape,
        compiler_params=pltpu.CompilerParams(vmem_limit_bytes=vmem * MIB),
        cost_estimate=pl.CostEstimate(
            flops=int(flops / SHARE),
            bytes_accessed=int(moved / SHARE),
            transcendentals=int(transcendentals / SHARE),
        ),
        **kwargs,
    )(*operands, *after)
    if chain:
        ORDER[:] = [made[0] if isinstance(made, (tuple, list)) else made]
    return made


def hold(values, after=()):
    n = len(values)
    made = lax.optimization_barrier((*values, *ORDER, *after))
    ORDER[:] = made[n : n + len(ORDER)]
    return list(made[:n])


def whole(memory):
    return pl.BlockSpec(memory_space=memory)


def rotated(values, cosine, signed):
    return values * cosine + pltpu.roll(values, HD // 2, 1) * signed


def unrotated(values, cosine, signed):
    return values * cosine - pltpu.roll(values, HD // 2, 1) * signed


def qkv_body(n, fresh, place_ref, *refs):
    if fresh:
        x_ref, gain_ref, refs = refs[0], refs[1], refs[2:]
    else:
        x_ref, refs = refs[0], refs[1:]
    wq_ref, wk_ref, wv_ref, cos_ref, sin_ref = refs[:5]
    outs, (w_s, x_s) = refs[5 : 5 + n], refs[-2:]
    step = pl.program_id(0)

    @pl.when(step == 0)
    def _():
        if fresh:
            x = x_ref[...].astype(F32)
            x_s[...] = (x * scale_of(x) * gain_ref[...]).astype(BF16)
            refs[5 + n][...] = x_s[...]
        else:
            x_s[...] = x_ref[...]

    w_s[:, :HD] = wq_ref[...]
    w_s[:, HD : 2 * HD] = wk_ref[...]
    w_s[:, 2 * HD :] = wv_ref[...]
    made = nn(x_s[...], w_s[...])
    cosine = cos_ref[...]
    signed = sin_ref[...]
    query = rotated(made[:, :HD], cosine, signed).astype(BF16)
    key = rotated(made[:, HD : 2 * HD], cosine, signed).astype(BF16)
    value = made[:, 2 * HD :].astype(BF16)
    for i in range(n):

        @pl.when(step == i)
        def _(i=i):
            outs[i][:, :HD] = query
            outs[i][:, HD : 2 * HD] = key
            outs[i][:, 2 * HD :] = value


def project_qkv(place, x, gain, weights, cosine, signed, spots):
    n = len(spots)
    rows, width = x.shape
    fresh = gain is not None
    fixed = pl.BlockSpec((rows, width), lambda i, place: (0, 0))
    table = pl.BlockSpec((rows, HD), lambda i, place: (0, 0))
    first = spots[0]
    assert list(spots) == [first ^ i for i in range(n)]
    weight = pl.BlockSpec((width, HD), lambda i, place: (0, place[0] ^ first ^ i))
    piece = jax.ShapeDtypeStruct((rows, 3 * HD), BF16)
    return call(
        functools.partial(qkv_body, n, fresh),
        (piece,) * n + ((jax.ShapeDtypeStruct(x.shape, BF16),) if fresh else ()),
        [place, x] + ([gain] if fresh else []) + [*weights, cosine, signed],
        [fixed]
        + ([pl.BlockSpec((1, width), lambda i, place: (0, 0))] if fresh else [])
        + [weight] * 3
        + [table] * 2,
        6 * n * rows * width * HD,
        4 * rows * width + 6 * n * width * HD + 6 * n * rows * HD,
        prefetch=1,
        grid=(n,),
        out_specs=(pl.BlockSpec((rows, 3 * HD), lambda i, place: (0, 0)),) * n
        + ((fixed,) if fresh else ()),
        scratch_shapes=[pltpu.VMEM((width, 3 * HD), BF16), pltpu.VMEM((rows, width), BF16)],
        vmem=60,
        name="project_qkv",
    )


def begin_of(index, ends_ref, count):
    begin = jnp.zeros_like(index)
    for e in range(count):
        end = ends_ref[e]
        begin = jnp.where(end <= index, jnp.maximum(begin, end), begin)
    return begin


def finish_of(index, ends_ref, count):
    finish = jnp.zeros_like(index) + ends_ref[count - 1]
    for e in range(count):
        end = ends_ref[e]
        finish = jnp.where(end > index, jnp.minimum(finish, end), finish)
    return finish


def attend_body(nz, ring, count, place_ref, ends_ref, *refs):
    n_kv = nz * ring
    q_refs, refs = refs[:nz], refs[nz:]
    kv_refs, refs = refs[:n_kv], refs[n_kv:]
    o_refs, refs = refs[:nz], refs[nz:]
    q_s, k_s, v_s, o_s, acc = refs
    z, r = place_ref[0], place_ref[1]
    rows = q_s.shape[1]
    for d in range(nz):
        q_s[d] = q_refs[d][:, :HD]
    for i in range(n_kv):
        first = kv_refs[i].shape[1] - 2 * HD
        k_s[i] = kv_refs[i][:, first : first + HD]
        v_s[i] = kv_refs[i][:, first + HD :]

    @pl.loop(0, nz)
    def per_query(d):
        q_block = (z ^ d) * ring + r
        q_start = q_block * rows
        q_index = q_start + lax.broadcasted_iota(jnp.int32, (rows, 1), 0)
        begin = begin_of(q_index, ends_ref, count)
        shift = jnp.log((finish_of(q_index, ends_ref, count) - begin).astype(F32))
        first_begin = begin_of(q_start, ends_ref, count)
        last_begin = begin_of(q_start + (rows - 1), ends_ref, count)
        acc[...] = jnp.zeros_like(acc)

        @pl.loop(0, n_kv)
        def per_key(i):
            k_block = (z ^ (i & (nz - 1))) * ring + (r ^ (i // nz))
            k_start = k_block * rows
            needed = (k_block <= q_block) & (k_start + rows > first_begin)
            full = (k_block < q_block) & (k_start >= last_begin)

            def tile(masked):
                half = rows // 2
                for part in range(2):
                    at = slice(part * half, (part + 1) * half)
                    scores = nt(q_s[d, at], k_s[i])
                    grown = jnp.exp(jnp.minimum(shift[at] - scores * FACTOR, CLAMP))
                    probs = pl.reciprocal(1.0 + grown, approx=True)
                    if masked:
                        k_index = k_start + lax.broadcasted_iota(jnp.int32, (1, rows), 1)
                        allowed = (k_index <= q_index[at]) & (k_index >= begin[at])
                        probs = jnp.where(allowed, probs, 0.0)
                    acc[at] += nn(probs.astype(BF16), v_s[i])

            pl.when(needed & full)(functools.partial(tile, False))
            pl.when(needed & jnp.logical_not(full))(functools.partial(tile, True))

        o_s[d] = acc[...].astype(BF16)

    for d in range(nz):
        o_refs[d][...] = o_s[d]


def attend(place, ends, queries, keys_values, nz, ring, after=()):
    rows = queries[0].shape[0]
    n_kv = nz * ring
    pairs = nz * n_kv / 2
    return call(
        functools.partial(attend_body, nz, ring, ends.shape[0]),
        tuple(jax.ShapeDtypeStruct((rows, HD), BF16) for _ in range(nz)),
        [place, ends, *queries, *keys_values],
        [whole(pltpu.SMEM)] * 2 + [whole(pltpu.VMEM)] * (nz + n_kv),
        pairs * 4 * rows * rows * HD * 2,
        2 * (2 * nz + 2 * n_kv) * rows * HD,
        pairs * 2 * rows * rows,
        after=after,
        out_specs=tuple(whole(pltpu.VMEM) for _ in range(nz)),
        scratch_shapes=[
            pltpu.VMEM((nz, rows, HD), BF16),
            pltpu.VMEM((n_kv, rows, HD), BF16),
            pltpu.VMEM((n_kv, rows, HD), BF16),
            pltpu.VMEM((nz, rows, HD), BF16),
            pltpu.VMEM((rows, HD), F32),
        ],
        vmem=12 + 2 * n_kv * rows * HD * 8 // MIB,
        name="attend",
    )


def attend_back_body(nz, ring, n_dr, first_dr, chained, count, place_ref, ends_ref, *refs):
    n_kv = nz * n_dr
    q_refs, refs = refs[:nz], refs[nz:]
    do_refs, refs = refs[:nz], refs[nz:]
    kv_refs, refs = refs[:n_kv], refs[n_kv:]
    if chained:
        before_ref, refs = refs[0], refs[1:]
    dq_ref, refs = refs[0], refs[1:]
    dkv_refs, refs = refs[:n_dr], refs[n_dr:]
    q_s, do_s, k_s, v_s, begin_s, shift_s, dkv_s, dk_acc, dv_acc = refs
    z, r = place_ref[0], place_ref[1]
    rows = q_s.shape[1]
    for d in range(nz):
        q_s[d] = q_refs[d][:, :HD]
        do_s[d] = do_refs[d][...]
    for i in range(n_kv):
        first = kv_refs[i].shape[1] - 2 * HD
        k_s[i] = kv_refs[i][:, first : first + HD]
        v_s[i] = kv_refs[i][:, first + HD :]
    if chained:
        dq_ref[...] = before_ref[...]
    else:
        dq_ref[...] = jnp.zeros_like(dq_ref)

    @pl.loop(0, nz)
    def tables(d):
        q_index = ((z ^ d) * ring + r) * rows + lax.broadcasted_iota(jnp.int32, (1, rows), 1)
        begin = begin_of(q_index, ends_ref, count)
        begin_s[d] = begin
        shift_s[d] = jnp.log((finish_of(q_index, ends_ref, count) - begin).astype(F32))

    @pl.loop(0, n_kv)
    def per_key(i):
        k_block = (z ^ (i & (nz - 1))) * ring + (r ^ (first_dr + i // nz))
        k_start = k_block * rows
        dk_acc[...] = jnp.zeros_like(dk_acc)
        dv_acc[...] = jnp.zeros_like(dv_acc)

        @pl.loop(0, nz)
        def per_query(d):
            q_block = (z ^ d) * ring + r
            q_start = q_block * rows
            first_begin = begin_of(q_start, ends_ref, count)
            last_begin = begin_of(q_start + (rows - 1), ends_ref, count)
            needed = (k_block <= q_block) & (k_start + rows > first_begin)
            full = (k_block < q_block) & (k_start >= last_begin)

            def tile(masked):
                half = rows // 2
                for part in range(2):
                    at = slice(part * half, (part + 1) * half)
                    keys = k_s[i, at]
                    scores = nt(keys, q_s[d])
                    grown = jnp.exp(jnp.minimum(shift_s[d] - scores * FACTOR, CLAMP))
                    probs = pl.reciprocal(1.0 + grown, approx=True)
                    if masked:
                        k_index = (
                            k_start
                            + part * half
                            + lax.broadcasted_iota(jnp.int32, (half, 1), 0)
                        )
                        q_index = q_start + lax.broadcasted_iota(jnp.int32, (1, rows), 1)
                        allowed = (k_index <= q_index) & (k_index >= begin_s[d])
                        probs = jnp.where(allowed, probs, 0.0)
                    weight_grad = nt(v_s[i, at], do_s[d])
                    score_grad = (weight_grad * (probs * probs * grown)).astype(BF16)
                    dv_acc[at] += nn(probs.astype(BF16), do_s[d])
                    dk_acc[at] += nn(score_grad, q_s[d])
                    dq_ref[d] += tn(score_grad, keys)

            pl.when(needed & full)(functools.partial(tile, False))
            pl.when(needed & jnp.logical_not(full))(functools.partial(tile, True))

        dkv_s[i, :, :HD] = (dk_acc[...] * FACTOR).astype(dkv_s.dtype)
        dkv_s[i, :, HD:] = dv_acc[...].astype(dkv_s.dtype)

    for e in range(n_dr):
        for d in range(nz):
            dkv_refs[e][d] = dkv_s[e * nz + d]


def attend_back(
    place, ends, queries, out_grads, keys_values, before, nz, ring, first_dr, n_dr, kept, after=()
):
    rows = queries[0].shape[0]
    n_kv = nz * n_dr
    pairs = nz * n_kv / 2
    chained = before is not None
    return call(
        functools.partial(
            attend_back_body, nz, ring, n_dr, first_dr, chained, ends.shape[0]
        ),
        (jax.ShapeDtypeStruct((nz, rows, HD), F32),)
        + tuple(jax.ShapeDtypeStruct((nz, rows, 2 * HD), kept) for _ in range(n_dr)),
        [place, ends, *queries, *out_grads, *keys_values, *([before] if chained else [])],
        [whole(pltpu.SMEM)] * 2 + [whole(pltpu.VMEM)] * (2 * nz + n_kv + chained),
        pairs * 10 * rows * rows * HD * 2,
        2 * (2 * nz + 4 * n_kv) * rows * HD,
        pairs * 2 * rows * rows,
        after=after,
        out_specs=tuple(whole(pltpu.VMEM) for _ in range(1 + n_dr)),
        scratch_shapes=[
            pltpu.VMEM((nz, rows, HD), BF16),
            pltpu.VMEM((nz, rows, HD), BF16),
            pltpu.VMEM((n_kv, rows, HD), BF16),
            pltpu.VMEM((n_kv, rows, HD), BF16),
            pltpu.VMEM((nz, 1, rows), jnp.int32),
            pltpu.VMEM((nz, 1, rows), F32),
            pltpu.VMEM((n_kv, rows, 2 * HD), kept),
            pltpu.VMEM((rows, HD), F32),
            pltpu.VMEM((rows, HD), F32),
        ],
        vmem=16 + 2 * n_kv * rows * HD * 14 // MIB,
        name="attend_back",
    )


def finish_body(nz, dq_ref, dkv_ref, got_ref, cos_ref, sin_ref, *out_refs):
    for d in range(nz):
        cosine = cos_ref[d]
        signed = sin_ref[d]
        total = dkv_ref[d] + got_ref[d].astype(F32)
        out = out_refs[d]
        out[:, :HD] = unrotated(dq_ref[d] * FACTOR, cosine, signed).astype(BF16)
        out[:, HD : 2 * HD] = unrotated(total[:, :HD], cosine, signed).astype(BF16)
        out[:, 2 * HD :] = total[:, HD:].astype(BF16)


def finish_grads(dq, dkv, got, cosine, signed):
    nz, rows, _ = dq.shape
    return call(
        functools.partial(finish_body, nz),
        tuple(jax.ShapeDtypeStruct((rows, 3 * HD), BF16) for _ in range(nz)),
        [dq, dkv, got, cosine, signed],
        [whole(pltpu.VMEM)] * 5,
        12 * nz * rows * HD,
        nz * rows * HD * 30,
        out_specs=tuple(whole(pltpu.VMEM) for _ in range(nz)),
        name="finish_grads",
    )


def rows_at(place, width, height, tile_of):
    return pl.BlockSpec((height, width), lambda j, place: (tile_of(place), 0))


def place_rows(pieces, scratch, spot):
    size = pieces[0].shape[0]
    half = size * len(pieces)
    for i, piece in enumerate(pieces):
        at = pl.multiple_of(spot * half + i * size, size)
        scratch[pl.ds(at, size), :] = piece[...]


def upstream_body(place_ref, *refs):
    pieces, (w_ref, out_ref, x_s) = refs[:-3], refs[-3:]
    size = pieces[0].shape[0]

    @pl.when(pl.program_id(0) == 0)
    def _():
        for i, piece in enumerate(pieces):
            x_s[i * size : (i + 1) * size] = piece[...]

    out_ref[...] = nt(x_s[...], w_ref[...]).astype(BF16)


def hidden_upstream(place, pieces, weights, own, after=()):
    size, width = pieces[0].shape
    rows = size * len(pieces)
    units = weights.shape[0] // (2 if own else 1)
    tile = 512
    steps = units // tile
    first = (lambda place: place[3] * steps) if own else (lambda place: 0)
    return call(
        upstream_body,
        jax.ShapeDtypeStruct((rows, units), BF16),
        [place, *pieces, weights],
        [pl.BlockSpec((size, width), lambda j, place: (0, 0))] * len(pieces)
        + [pl.BlockSpec((tile, width), lambda j, place: (first(place) + j, 0))],
        2 * rows * width * units,
        2 * width * units + 4 * rows * units + 2 * rows * width,
        after=after,
        prefetch=1,
        grid=(steps,),
        out_specs=pl.BlockSpec((rows, tile), lambda j, place: (0, j)),
        scratch_shapes=[pltpu.VMEM((rows, width), BF16)],
        vmem=52,
        name="hidden_upstream",
    )


def hidden_body(place_ref, *refs):
    pieces, refs = refs[:-7], refs[-7:]
    wg_ref, wu_ref, dact_ref, act_ref, dg_ref, du_ref, x_s = refs
    size = pieces[0].shape[0]

    @pl.when(pl.program_id(0) == 0)
    def _():
        for i, piece in enumerate(pieces):
            x_s[i * size : (i + 1) * size] = piece[...]

    x = x_s[...]
    for first in range(0, act_ref.shape[1], 256):
        at = slice(first, first + 256)
        gate = nn(x, wg_ref[:, at])
        up = nn(x, wu_ref[:, at])
        dact = dact_ref[:, at].astype(F32)
        sig = jax.nn.sigmoid(gate)
        silu = gate * sig
        act_ref[:, at] = (silu * up).astype(BF16)
        dg_ref[:, at] = (dact * up * sig * (1.0 + gate * (1.0 - sig))).astype(BF16)
        du_ref[:, at] = (dact * silu).astype(BF16)


def hidden(place, pieces, w_gate, w_up, dact, own, after=()):
    size, width = pieces[0].shape
    rows = size * len(pieces)
    units = dact.shape[1]
    tile = 512
    steps = units // tile
    first = (lambda place: place[3] * steps) if own else (lambda place: 0)
    made = jax.ShapeDtypeStruct((rows, units), BF16)
    block = pl.BlockSpec((rows, tile), lambda j, place: (0, j))
    weight = pl.BlockSpec((width, tile), lambda j, place: (0, first(place) + j))
    return call(
        hidden_body,
        (made, made, made),
        [place, *pieces, w_gate, w_up, dact],
        [pl.BlockSpec((size, width), lambda j, place: (0, 0))] * len(pieces)
        + [weight, weight, block],
        4 * rows * width * units,
        4 * width * units + 8 * rows * units + 2 * rows * width,
        rows * units,
        after=after,
        prefetch=1,
        grid=(steps,),
        out_specs=(block, block, block),
        scratch_shapes=[pltpu.VMEM((rows, width), BF16)],
        vmem=52,
        name="hidden",
    )


def chunked(total, out_refs):
    size = out_refs[0].shape[0]
    for i, ref in enumerate(out_refs):
        ref[...] = total[i * size : (i + 1) * size].astype(ref.dtype)


def back_body(place_ref, dg_ref, dg_sib, du_ref, du_sib, wg_ref, wg_sib, wu_ref, wu_sib, *outs):
    chunked(
        nt(dg_ref[...], wg_ref[...])
        + nt(dg_sib[...], wg_sib[...])
        + nt(du_ref[...], wu_ref[...])
        + nt(du_sib[...], wu_sib[...]),
        outs,
    )


def hidden_back(place, dg, dg_sib, du, du_sib, w_gate, gate_sib, w_up, up_sib, chunks, after=()):
    rows, half = dg.shape
    width = w_gate.shape[0]
    tile = 512
    size = rows // chunks
    left = pl.BlockSpec((rows, half), lambda j, place: (0, 0))
    own = pl.BlockSpec((tile, half), lambda j, place: (j, place[3]))
    sib = pl.BlockSpec((tile, half), lambda j, place: (j, 0))
    return call(
        back_body,
        tuple(jax.ShapeDtypeStruct((size, width), BF16) for _ in range(chunks)),
        [place, dg, dg_sib, du, du_sib, w_gate, gate_sib, w_up, up_sib],
        [left] * 4 + [own, sib, own, sib],
        8 * rows * width * half,
        8 * width * half + 8 * rows * half + 2 * rows * width,
        after=after,
        prefetch=1,
        grid=(width // tile,),
        out_specs=tuple(pl.BlockSpec((size, tile), lambda j, place: (0, j)) for _ in range(chunks)),
        vmem=52,
        name="hidden_back",
    )


def down_body(place_ref, act_ref, act_sib, wd_ref, wd_sib, *outs):
    chunked(nn(act_ref[...], wd_ref[...]) + nn(act_sib[...], wd_sib[...]), outs)


def down(place, act, act_sib, w_down, down_sib, chunks, after=()):
    rows, half = act.shape
    width = w_down.shape[1]
    tile = 512
    size = rows // chunks
    left = pl.BlockSpec((rows, half), lambda j, place: (0, 0))
    return call(
        down_body,
        tuple(jax.ShapeDtypeStruct((size, width), BF16) for _ in range(chunks)),
        [place, act, act_sib, w_down, down_sib],
        [
            left,
            left,
            pl.BlockSpec((half, tile), lambda j, place: (place[3], j)),
            pl.BlockSpec((half, tile), lambda j, place: (0, j)),
        ],
        4 * rows * width * half,
        4 * width * half + 4 * rows * half + 2 * rows * width,
        after=after,
        prefetch=1,
        grid=(width // tile,),
        out_specs=tuple(pl.BlockSpec((size, tile), lambda j, place: (0, j)) for _ in range(chunks)),
        vmem=52,
        name="down",
    )


def heads_body(nz, contract, keep, place_ref, *refs):
    n_w = 1 if keep else 3
    pieces, refs = refs[:nz], refs[nz:]
    w_refs, (sib_ref, mine_ref), refs = refs[:n_w], refs[n_w : n_w + 2], refs[n_w + 2 :]
    joined = refs[:n_w]
    for d in range(nz):
        at = pl.multiple_of((place_ref[0] ^ d) * HD, HD)
        for i in range(n_w):
            joined[i][:, pl.ds(at, HD)] = pieces[d][:, i * HD : (i + 1) * HD]
    half = sib_ref.shape[0]
    core = place_ref[2] & 1

    def rows_of(start):
        start = pl.multiple_of(start, half)
        total = contract(joined[0][pl.ds(start, half), :], w_refs[0][...])
        for i in range(1, n_w):
            total = total + contract(joined[i][pl.ds(start, half), :], w_refs[i][...])
        return total

    sib_ref[...] = rows_of((1 - core) * half).astype(BF16)
    mine_ref[...] = rows_of(core * half)


def heads_project(place, pieces, weights, contract, keep, after=()):
    nz = len(pieces)
    rows = pieces[0].shape[0]
    n_w = len(weights)
    width = weights[0].shape[1] if contract is nn else weights[0].shape[0]
    half = rows // 2
    joined = (rows, nz * HD)
    out = (
        jax.ShapeDtypeStruct((half, width), BF16),
        jax.ShapeDtypeStruct((half, width), F32),
    ) + ((jax.ShapeDtypeStruct(joined, BF16),) if keep else ())
    return call(
        functools.partial(heads_body, nz, contract, keep),
        out,
        [place, *pieces, *weights],
        [whole(pltpu.SMEM)] + [whole(pltpu.VMEM)] * (nz + n_w),
        2 * rows * width * nz * HD * n_w,
        2 * n_w * (width * nz * HD + rows * nz * HD) + 3 * rows * width,
        after=after,
        out_specs=tuple(whole(pltpu.VMEM) for _ in out),
        scratch_shapes=() if keep else (pltpu.VMEM(joined, BF16),) * n_w,
        vmem=24,
        name="heads_project",
    )


def dheads_body(nz, n, place_ref, *refs):
    mine, refs = refs[:n], refs[n:]
    sibs, refs = refs[:n], refs[n:]
    w_ref, outs, x_s = refs[0], refs[1:-1], refs[-1]
    core = place_ref[2] & 1
    place_rows(mine, x_s, core)
    place_rows(sibs, x_s, 1 - core)
    x = x_s[...]
    wide = outs[0].shape[1]
    for d in range(nz):
        at = pl.multiple_of((place_ref[0] ^ d) * wide, wide)
        outs[d][...] = nt(x, w_ref[pl.ds(at, wide), :]).astype(BF16)


def heads_upstream(place, mine, sibs, w_out, nz, after=()):
    n = len(mine)
    size, width = mine[0].shape
    rows = 2 * n * size
    wide = w_out.shape[0] // nz
    return call(
        functools.partial(dheads_body, nz, n),
        tuple(jax.ShapeDtypeStruct((rows, wide), BF16) for _ in range(nz)),
        [place, *mine, *sibs, w_out],
        [whole(pltpu.SMEM)] + [whole(pltpu.VMEM)] * (2 * n + 1),
        2 * rows * width * nz * wide,
        2 * width * nz * wide + 2 * rows * nz * wide + 2 * rows * width,
        after=after,
        out_specs=tuple(whole(pltpu.VMEM) for _ in range(nz)),
        scratch_shapes=[pltpu.VMEM((rows, width), BF16)],
        name="heads_upstream",
    )


def sum_body(mine_ref, got_ref, *outs):
    chunked(mine_ref[...].astype(F32) + got_ref[...].astype(F32), outs)


def row_sum(mine, got, chunks, after=()):
    rows, width = mine.shape
    size = rows // chunks
    return call(
        sum_body,
        tuple(jax.ShapeDtypeStruct((size, width), BF16) for _ in range(chunks)),
        [mine, got],
        [whole(pltpu.VMEM)] * 2,
        rows * width,
        8 * rows * width,
        after=after,
        out_specs=tuple(whole(pltpu.VMEM) for _ in range(chunks)),
        name="row_sum",
    )


def scale_of(values):
    return lax.rsqrt(jnp.mean(values * values, axis=-1, keepdims=True) + EPSILON)


def norm_body(part_ref, got_ref, x_ref, gain_ref, res_ref, normed_ref):
    residual = x_ref[...].astype(F32) + (part_ref[...].astype(F32) + got_ref[...].astype(F32))
    res_ref[...] = residual
    normed_ref[...] = (residual * scale_of(residual) * gain_ref[...]).astype(BF16)


def norm_rows(part, got, x, gain, after=()):
    rows, width = part.shape
    return call(
        norm_body,
        (
            jax.ShapeDtypeStruct((rows, width), F32),
            jax.ShapeDtypeStruct((rows, width), BF16),
        ),
        [part, got, x, gain],
        [whole(pltpu.VMEM)] * 4,
        8 * rows * width,
        12 * rows * width,
        after=after,
        out_specs=(whole(pltpu.VMEM), whole(pltpu.VMEM)),
        name="norm_rows",
    )


def norm_back_body(part_ref, got_ref, values_ref, add_ref, gain_ref, *outs):
    upstream = part_ref[...].astype(F32) + got_ref[...].astype(F32)
    values = values_ref[...].astype(F32)
    scale = scale_of(values)
    normed = values * scale
    outs[-1][...] = jnp.sum(upstream * normed, axis=0, keepdims=True)
    weighted = upstream * gain_ref[...]
    grad = scale * (weighted - normed * jnp.mean(weighted * normed, axis=-1, keepdims=True))
    total = add_ref[...].astype(F32) + grad
    for ref in outs[:-1]:
        ref[...] = total.astype(ref.dtype)


def norm_back(part, got, values, add, gain, kinds, after=()):
    rows, width = part.shape
    return call(
        norm_back_body,
        tuple(jax.ShapeDtypeStruct((rows, width), kind) for kind in kinds)
        + (jax.ShapeDtypeStruct((1, width), F32),),
        [part, got, values, add, gain],
        [whole(pltpu.VMEM)] * 5,
        16 * rows * width,
        16 * rows * width,
        after=after,
        out_specs=tuple(whole(pltpu.VMEM) for _ in range(len(kinds) + 1)),
        name="norm_back",
    )


def add_body(part_ref, got_ref, res_ref, out_ref):
    out_ref[...] = (
        res_ref[...] + (part_ref[...].astype(F32) + got_ref[...].astype(F32))
    ).astype(BF16)


def add_rows(part, got, residual, after=()):
    return call(
        add_body,
        jax.ShapeDtypeStruct(part.shape, BF16),
        [part, got, residual],
        [whole(pltpu.VMEM)] * 3,
        part.size,
        10 * part.size,
        after=after,
        out_specs=whole(pltpu.VMEM),
        name="add_rows",
    )


def join_body(n, place_ref, *refs):
    core = place_ref[2] & 1
    place_rows(refs[:n], refs[-1], core)
    place_rows(refs[n : 2 * n], refs[-1], 1 - core)


def join_rows(place, mine, sibs, after=()):
    n = len(mine)
    size, width = mine[0].shape
    return call(
        functools.partial(join_body, n),
        jax.ShapeDtypeStruct((2 * n * size, width), BF16),
        [place, *mine, *sibs],
        [whole(pltpu.SMEM)] + [whole(pltpu.VMEM)] * (2 * n),
        0,
        8 * n * size * width,
        after=after,
        out_specs=whole(pltpu.VMEM),
        name="join_rows",
    )


def turn_body(n, block, offset_ref, order_ref, *refs):
    pieces, out_ref = refs[:n], refs[n]
    size, wide = pieces[0].shape
    unit = (
        lax.broadcasted_iota(jnp.int32, (block, block), 0)
        == lax.broadcasted_iota(jnp.int32, (block, block), 1)
    ).astype(F32).astype(BF16)
    for p in range(wide // block):
        at = pl.multiple_of(order_ref[p] * block, block)
        for j in range(n):
            to = pl.multiple_of(offset_ref[j] * size, size)
            made = nt(unit, pieces[j][:, pl.ds(at, block)]).astype(BF16)
            out_ref[p * block : (p + 1) * block, pl.ds(to, size)] = made


def turn(order, group, pieces, offsets=None, after=()):
    wide = pieces[0].shape[1]
    if group % 128 != 0:
        pieces = [
            jnp.concatenate(
                [
                    lax.dynamic_slice_in_dim(piece, order[p] * group, group, 1)
                    for p in range(order.shape[0])
                ],
                axis=1,
            )
            for piece in pieces
        ]
        block = math.gcd(256, wide)
        order_in = jnp.arange(wide // block, dtype=jnp.int32)
    else:
        block = group
        order_in = order
    n = len(pieces)
    size = pieces[0].shape[0]
    tokens = n * size
    if offsets is None:
        offsets = jnp.arange(n, dtype=jnp.int32)
    return call(
        functools.partial(turn_body, n, block),
        jax.ShapeDtypeStruct((wide, tokens), BF16),
        [offsets, order_in, *pieces],
        [whole(pltpu.SMEM)] * 2 + [whole(pltpu.VMEM)] * n,
        2 * tokens * wide * block,
        4 * tokens * wide,
        after=after,
        out_specs=whole(pltpu.VMEM),
        vmem=8 + 4 * tokens * wide // MIB,
        name="turn",
    )


def stack_body(*refs):
    for i, ref in enumerate(refs[:-1]):
        refs[-1][i] = ref[...]


def stack_rows(pieces):
    n = len(pieces)
    return call(
        stack_body,
        jax.ShapeDtypeStruct((n, *pieces[0].shape), BF16),
        list(pieces),
        [whole(pltpu.VMEM)] * n,
        0,
        4 * n * pieces[0].size,
        out_specs=whole(pltpu.VMEM),
        name="stack_rows",
    )


def turn_all_body(block, place_ref, order_ref, own_ref, *refs):
    parts, out_ref = refs[:-1], refs[-1]
    n = len(parts)
    size, wide = parts[0].shape[1:]
    unit = (
        lax.broadcasted_iota(jnp.int32, (block, block), 0)
        == lax.broadcasted_iota(jnp.int32, (block, block), 1)
    ).astype(F32).astype(BF16)

    @pl.when(pl.program_id(0) == 0)
    def _():
        for p in range(wide // block):
            at = pl.multiple_of(order_ref[p] * block, block)
            made = nt(unit, own_ref[:, pl.ds(at, block)]).astype(BF16)
            out_ref[p * block : (p + 1) * block, :] = made

    @pl.when(pl.program_id(0) > 0)
    def _():
        for p in range(wide // block):
            at = pl.multiple_of(order_ref[p] * block, block)
            for j in range(n):
                to = pl.multiple_of((place_ref[0] ^ j) * size, size)
                made = nt(unit, parts[j][0, :, pl.ds(at, block)]).astype(BF16)
                out_ref[p * block : (p + 1) * block, pl.ds(to, size)] = made


def turn_all(order, group, own, parts, m):
    tokens, wide = own.shape
    others, size, _ = parts[0].shape
    if group % 128 != 0:

        def ordered(values):
            axis = values.ndim - 1
            return jnp.concatenate(
                [
                    lax.dynamic_slice_in_dim(values, order[p] * group, group, axis)
                    for p in range(order.shape[0])
                ],
                axis=axis,
            )

        own = ordered(own)
        parts = [ordered(part) for part in parts]
        block = math.gcd(256, wide)
        order_in = jnp.arange(wide // block, dtype=jnp.int32)
    else:
        block = group
        order_in = order
    return call(
        functools.partial(turn_all_body, block),
        jax.ShapeDtypeStruct((wide, (others + 1) * tokens), BF16),
        [m.reshape(1).astype(jnp.int32), order_in, own, *parts],
        [pl.BlockSpec((tokens, wide), lambda d, place, order: (0, 0))]
        + [
            pl.BlockSpec((1, size, wide), lambda d, place, order: (jnp.maximum(d - 1, 0), 0, 0))
        ]
        * len(parts),
        2 * (others + 1) * tokens * wide * block,
        4 * (others + 1) * tokens * wide,
        prefetch=2,
        grid=(others + 1,),
        out_specs=pl.BlockSpec((wide, tokens), lambda d, place, order: (0, d)),
        vmem=52,
        name="turn_all",
    )


def weight_body(n, *refs):
    lefts, refs = refs[:n], refs[n:]
    rights, (sent_ref, kept_ref) = refs[:n], refs[n:]
    total = nn(lefts[0][...], rights[0][...])
    for i in range(1, n):
        total = total + nn(lefts[i][...], rights[i][...])
    half = pl.num_programs(0) // 2

    @pl.when(pl.program_id(0) < half)
    def _():
        sent_ref[...] = total.astype(BF16)

    @pl.when(pl.program_id(0) >= half)
    def _():
        kept_ref[...] = total.astype(BF16)


def weight_grad(lefts, rights, after=()):
    wide = lefts[0].shape[0]
    width = rights[0].shape[1]
    tokens = sum(left.shape[1] for left in lefts)
    steps = 4
    tile = wide // steps
    half = steps // 2
    made = jax.ShapeDtypeStruct((wide // 2, width), BF16)
    return call(
        functools.partial(weight_body, len(lefts)),
        (made,) * 2,
        [*lefts, *rights],
        [
            pl.BlockSpec((tile, left.shape[1]), lambda i: ((i + half) % steps, 0))
            for left in lefts
        ]
        + [pl.BlockSpec(right.shape, lambda i: (0, 0)) for right in rights],
        2 * tokens * wide * width,
        2 * (tokens * wide + tokens * width + wide * width),
        after=after,
        grid=(steps,),
        out_specs=(
            pl.BlockSpec((tile, width), lambda i: (jnp.minimum(i, half - 1), 0)),
            pl.BlockSpec((tile, width), lambda i: (jnp.maximum(i - half, 0), 0)),
        ),
        vmem=52,
        name="weight_grad",
    )


def sum3_body(n, *refs):
    total = refs[0][...].astype(F32)
    for ref in refs[1:n]:
        total = total + ref[...].astype(F32)
    low_ref, high_ref = refs[n:]
    low_ref[...] = total[0]
    high_ref[...] = total[1].astype(BF16)


def final_sum(terms, after=()):
    wide, width = terms[0].shape
    high = wide // 2
    tile = math.gcd(high, 128)
    block = pl.BlockSpec((2, tile, width), lambda i: (0, i, 0))
    out = pl.BlockSpec((tile, width), lambda i: (i, 0))
    return call(
        functools.partial(sum3_body, len(terms)),
        (
            jax.ShapeDtypeStruct((high, width), F32),
            jax.ShapeDtypeStruct((high, width), BF16),
        ),
        [term.reshape(2, high, width) for term in terms],
        [block] * len(terms),
        wide * width,
        wide * width * 8,
        after=after,
        grid=(high // tile,),
        out_specs=(out, out),
        name="final_sum",
    )


def merge_body(kept_ref, got_ref, low_ref, high_ref):
    total = kept_ref[...].astype(F32) + got_ref[...].astype(F32)
    low_ref[...] = total[0]
    high_ref[...] = total[1].astype(BF16)


def merge(kept, got, after=()):
    wide, width = kept.shape
    high = wide // 2
    tile = math.gcd(high, 128)
    operands = [kept.reshape(2, high, width), got.reshape(2, high, width)]
    block = pl.BlockSpec((2, tile, width), lambda i: (0, i, 0))
    out = pl.BlockSpec((tile, width), lambda i: (i, 0))
    return call(
        merge_body,
        (
            jax.ShapeDtypeStruct((high, width), F32),
            jax.ShapeDtypeStruct((high, width), BF16),
        ),
        operands,
        [block, block],
        wide * width,
        wide * width * 8,
        after=after,
        grid=(high // tile,),
        out_specs=(out, out),
        name="merge",
    )


def lay_body(turned, place_ref, own_ref, got_ref, out_ref):
    value = jnp.where(pl.program_id(0) == 0, own_ref[...], got_ref[...].astype(F32))
    out_ref[...] = value.T if turned else value


def lay(place, own, got, turned):
    rows, width = own.shape
    if turned:
        shape, block = (2 * width, rows), (width, rows)
        index = lambda i, place: (place[3] ^ i, 0)
    else:
        shape, block = (rows, 2 * width), (rows, width)
        index = lambda i, place: (0, place[3] ^ i)
    fixed = pl.BlockSpec((rows, width), lambda i, place: (0, 0))
    return call(
        functools.partial(lay_body, turned),
        jax.ShapeDtypeStruct(shape, F32),
        [place, own, got],
        [fixed, fixed],
        0,
        14 * rows * width,
        prefetch=1,
        grid=(2,),
        out_specs=pl.BlockSpec(block, index),
        name="lay",
    )


def qkv_sum_body(kept_ref, got_ref, own_ref, *outs):
    size = own_ref.shape[0]
    total = kept_ref[...].astype(F32) + got_ref[...].astype(F32)
    own_ref[...] = total[:size]
    for i, ref in enumerate(outs):
        ref[...] = total[(i + 1) * size : (i + 2) * size].astype(BF16)


def split_sum(kept, got, n):
    rows, width = kept.shape
    size = rows // n
    return call(
        qkv_sum_body,
        (jax.ShapeDtypeStruct((size, width), F32),)
        + (jax.ShapeDtypeStruct((size, width), BF16),) * (n - 1),
        [kept, got],
        [whole(pltpu.VMEM)] * 2,
        rows * width,
        8 * rows * width,
        out_specs=(whole(pltpu.VMEM),) * n,
        name="split_sum",
    )


def place_heads_body(nz, place_ref, *refs):
    pieces, outs = refs[:nz], refs[nz:]
    for d in range(nz):
        at = pl.multiple_of((place_ref[0] ^ d) * HD, HD)
        for i, out in enumerate(outs):
            out[:, pl.ds(at, HD)] = pieces[d][:, i * HD : (i + 1) * HD].astype(F32)


def place_heads(place, pieces):
    nz = len(pieces)
    rows = pieces[0].shape[0]
    return call(
        functools.partial(place_heads_body, nz),
        (jax.ShapeDtypeStruct((rows, nz * HD), F32),) * 3,
        [place, *pieces],
        [whole(pltpu.SMEM)] + [whole(pltpu.VMEM)] * nz,
        0,
        20 * rows * nz * HD,
        out_specs=(whole(pltpu.VMEM),) * 3,
        name="place_heads",
    )


def rope_tables(position):
    middle = HD // 2
    frequency = THETA ** (-(jnp.arange(middle, dtype=F32) * 2.0 / HD))
    angles = position.astype(F32)[..., None] * frequency
    cosine = jnp.cos(angles)
    sine = jnp.sin(angles)
    return (
        jnp.concatenate([cosine, cosine], axis=-1),
        jnp.concatenate([-sine, sine], axis=-1),
    )


def rms_scale(values):
    return lax.rsqrt(jnp.mean(values * values, axis=-1, keepdims=True) + EPSILON)


def layer(
    n_seq,
    n_mp,
    mixed_in,
    w_query,
    w_key,
    w_value,
    w_out,
    gain_attn,
    w_gate,
    w_up,
    w_down,
    gain_mlp,
    doc_ends,
    cotangent,
):
    rows, width = mixed_in.shape
    nz = w_query.shape[1] // HD
    ring = n_seq // nz
    bits = n_seq.bit_length() - 1
    low_bits = ring.bit_length() - 1
    units = w_gate.shape[1]
    half_units = units // 2
    half_rows = rows // 2
    group = width // n_seq
    pair_bit = bits - 2
    pair = 1 << pair_bit

    s = lax.axis_index("seq")
    m = lax.axis_index("mp")
    z, r = s // ring, s % ring
    core = m % 2
    side = m // 2
    low = (s >> pair_bit) & 1

    def seq_swap(v, distance):
        return lax.ppermute(v, "seq", [(i, i ^ distance) for i in range(n_seq)])

    def mp_swap(v, distance):
        return lax.ppermute(v, "mp", [(i, i ^ distance) for i in range(n_mp)])

    sum_bits = list(range(pair_bit)) + [bits - 1]
    places = []
    for p in range(n_seq):
        e = 0
        for at, bit in enumerate(sum_bits + [pair_bit]):
            if (p >> (bits - 1 - at)) & 1:
                e |= 1 << bit
        places.append(e)
    order = s ^ jnp.array(places, dtype=jnp.int32)

    ORDER.clear()

    place = jnp.stack([z, r, m, low]).astype(jnp.int32)
    blocks = (z ^ jnp.arange(nz, dtype=jnp.int32)) * ring + r
    token_index = blocks[:, None] * rows + jnp.arange(rows, dtype=jnp.int32)[None, :]
    ends_below = doc_ends[None, None, :] <= token_index[..., None]
    begin = jnp.max(jnp.where(ends_below, doc_ends, 0), axis=-1)
    cos_own, sin_own = rope_tables(token_index[0] - begin[0])
    weights = [w_query, w_key, w_value]
    half_z = nz // 2
    made = project_qkv(
        place,
        mixed_in,
        gain_attn.reshape(1, width),
        weights,
        cos_own,
        sin_own,
        list(range(half_z, nz)),
    )
    normed = made[-1]
    pieces = {half_z + i: made[i] for i in range(half_z)}
    made = project_qkv(place, normed, None, weights, cos_own, sin_own, list(range(half_z)))
    pieces.update({i: made[i] for i in range(half_z)})
    pieces = [pieces[0]] + [seq_swap(pieces[d], d * ring) for d in range(1, nz)]
    near = pieces
    keys_values = [near, [seq_swap(piece[:, HD:], 1) for piece in pieces]]
    for b in range(1, low_bits):
        keys_values = keys_values + [
            [seq_swap(kv[:, -2 * HD :], 1 << b) for kv in kvs] for kvs in keys_values
        ]
    queries = pieces

    quarter = rows // n_mp
    my_quarter = lax.dynamic_slice_in_dim(normed, m * quarter, quarter, 0)
    halves = [
        lax.dynamic_slice_in_dim(w_down, low * half_units, half_units, 0),
        lax.dynamic_slice_in_dim(w_gate, low * half_units, half_units, 1),
        lax.dynamic_slice_in_dim(w_up, low * half_units, half_units, 1),
    ]
    cot_half = lax.dynamic_slice_in_dim(cotangent, core * half_rows, half_rows, 0)

    flat = [kv for kvs in keys_values for kv in kvs]
    far = [kv for kvs in keys_values[1:] for kv in kvs]
    cot_half, *halves = hold([cot_half, *halves], after=pieces)
    cot_pair = seq_swap(cot_half, pair)
    outs = attend(place, doc_ends, queries, flat, nz, ring)
    heads = [outs[0]] + [seq_swap(outs[d], d * ring) for d in range(1, nz)]

    size = half_rows // CHUNKS
    last_low = 1 << sum_bits[pair_bit - 1]
    high = 1 << sum_bits[pair_bit]
    gain_mlp_row = gain_mlp.reshape(1, width)
    gain_attn_row = gain_attn.reshape(1, width)

    def chunks_of(values):
        return [values[i * size : (i + 1) * size] for i in range(CHUNKS)]

    def low_sums(sent, kept):
        for bit in sum_bits[: pair_bit - 1]:
            kept, sent = merge(kept, seq_swap(sent, 1 << bit))
        return kept, seq_swap(sent, last_low)

    x_chunks = chunks_of(lax.dynamic_slice_in_dim(mixed_in, core * half_rows, half_rows, 0))
    cot_chunks = chunks_of(cot_half)
    cot_all = cot_chunks + chunks_of(cot_pair)
    spots = jnp.concatenate(
        [core * CHUNKS + jnp.arange(CHUNKS), (1 - core) * CHUNKS + jnp.arange(CHUNKS)]
    ).astype(jnp.int32)
    v = types.SimpleNamespace(
        residual=[None] * CHUNKS,
        normed=[None] * (2 * CHUNKS),
        back=[None] * CHUNKS,
        back_across=[None] * CHUNKS,
        residual_grad=[None] * CHUNKS,
        branch=[None] * CHUNKS,
        branch_sib=[None] * CHUNKS,
        gain_mlp=[None] * CHUNKS,
        gain_attn=[None] * CHUNKS,
        grad_rows=[None] * CHUNKS,
        grad_sib=[None] * CHUNKS,
        quarters={0: my_quarter},
        out_grads=(),
    )
    def heads_out():
        sib, v.mine, v.heads_placed = heads_project(
            place, heads, [w_out], nn, True, after=[cot_pair]
        )
        v.sib = mp_swap(sib, 1)

    def out_sum():
        v.parts = row_sum(v.mine, v.sib, CHUNKS)
        v.across = [mp_swap(part, 2) for part in v.parts]

    def swap_weights():
        v.down_sib, v.gate_sib, v.up_sib = [mp_swap(half, 1) for half in hold(halves)]

    def dact_own():
        v.dact = hidden_upstream(place, cot_all, w_down, True)

    def dact_sib():
        v.dact_sib = hidden_upstream(place, cot_all, v.down_sib, False)

    def norm_chunk(i):
        v.residual[i], v.normed[i] = norm_rows(
            v.parts[i], v.across[i], x_chunks[i], gain_mlp_row
        )
        v.normed[CHUNKS + i] = seq_swap(v.normed[i], pair)

    def turn_cot():
        v.cot_turned = turn(order, group, cot_all)

    def swap_cot():
        (turned,) = hold([v.cot_turned])
        v.cot_both = [turned, mp_swap(turned, 1)]

    def hidden_sib():
        v.act_sib, dg_sib, du_sib = hidden(
            place, v.normed, v.gate_sib, v.up_sib, v.dact_sib, False
        )
        v.act_got = mp_swap(v.act_sib, 1)
        v.dg_sib, v.du_sib = dg_sib, du_sib

    def swap_dg():
        (part,) = hold([v.dg_sib])
        v.dg_got = mp_swap(part, 1)

    def swap_du():
        (part,) = hold([v.du_sib])
        v.du_got = mp_swap(part, 1)

    def hidden_own():
        v.act, v.dg, v.du = hidden(place, v.normed, w_gate, w_up, v.dact, True)

    def turn_normed():
        v.normed_turned = turn(order, group, v.normed)

    def swap_normed():
        (turned,) = hold([v.normed_turned])
        v.normed_both = [turned, mp_swap(turned, 1)]

    def grad_down():
        v.sent_down, v.part_down = weight_grad(v.cot_both, [v.act, v.act_got])

    def send_down():
        (sent,) = hold([v.sent_down])
        v.low_down = low_sums(sent, v.part_down)

    def hidden_in():
        v.made = hidden_back(
            place,
            v.dg,
            v.dg_sib,
            v.du,
            v.du_sib,
            w_gate,
            v.gate_sib,
            w_up,
            v.up_sib,
            2 * CHUNKS,
        )
        v.made_got = [seq_swap(v.made[CHUNKS + i], pair) for i in range(CHUNKS)]

    def back_chunk(i):
        (v.back[i],) = row_sum(v.made[i], v.made_got[i], 1)
        v.back_across[i] = mp_swap(v.back[i], 2)

    def norm_back_chunk(i):
        v.residual_grad[i], v.branch[i], v.gain_mlp[i] = norm_back(
            v.back[i], v.back_across[i], v.residual[i], cot_chunks[i], gain_mlp_row, (F32, BF16)
        )
        v.branch_sib[i] = mp_swap(v.branch[i], 1)

    def grad_gate():
        v.sent_gate, v.part_gate = weight_grad(v.normed_both, [v.dg, v.dg_got])

    def send_gate():
        (sent,) = hold([v.sent_gate])
        v.low_gate = low_sums(sent, v.part_gate)

    def grad_up():
        v.sent_up, v.part_up = weight_grad(v.normed_both, [v.du, v.du_got])

    def send_up():
        (sent,) = hold([v.sent_up])
        v.low_up = low_sums(sent, v.part_up)

    def merge_down():
        v.kept_down, v.high_down = merge(*v.low_down)

    def high_down():
        (sent,) = hold([v.high_down], after=v.out_grads)
        v.come_down = seq_swap(sent, high)

    def merge_gate():
        v.kept_gate, v.high_gate = merge(*v.low_gate)

    def high_gate():
        (sent,) = hold([v.high_gate])
        v.come_gate = seq_swap(sent, high)

    def merge_up():
        v.kept_up, v.high_up = merge(*v.low_up)

    def high_up():
        (sent,) = hold([v.high_up])
        v.come_up = seq_swap(sent, high)

    def sum_down():
        v.own_down, v.pair_down = final_sum([v.kept_down, v.come_down])

    def sum_gate():
        v.own_gate, v.pair_gate = final_sum([v.kept_gate, v.come_gate])

    def sum_up():
        v.own_up, v.pair_up = final_sum([v.kept_up, v.come_up])

    def pair_down():
        (sent,) = hold([v.pair_down])
        v.theirs_down = seq_swap(sent, pair)

    def pair_gate():
        (sent,) = hold([v.pair_gate])
        v.theirs_gate = seq_swap(sent, pair)

    def pair_up():
        (sent,) = hold([v.pair_up])
        v.theirs_up = seq_swap(sent, pair)

    def lay_down():
        v.down_share = lay(place, v.own_down, v.theirs_down, True)

    def lay_gate():
        v.gate_share = lay(place, v.own_gate, v.theirs_gate, False)

    def lay_up():
        v.up_share = lay(place, v.own_up, v.theirs_up, False)

    def gather_z(d):
        (part,) = hold([v.quarters[d & (d - 1)]])
        v.quarters[d] = seq_swap(part, ring * (d & -d))

    def gather_x():
        v.rows = stack_rows([v.quarters[d] for d in range(1, nz)])
        v.rows_x = mp_swap(v.rows, 2)

    def gather_core():
        v.rows_core = [mp_swap(part, 1) for part in hold([v.rows, v.rows_x])]

    def heads_in():
        made = heads_upstream(place, v.branch, v.branch_sib, w_out, nz)
        v.out_grads = [made[0]] + [seq_swap(made[d], d * ring) for d in range(1, nz)]

    def attend_far():
        v.dq_far, *summed = attend_back(
            place, doc_ends, queries, v.out_grads, far, None, nz, ring, 1, ring - 1, BF16
        )
        summed = [None] + summed
        for b in reversed(range(low_bits)):
            bit = 1 << b
            for e in range(bit):
                got = seq_swap(summed[e | bit], bit)
                summed[e] = (
                    got
                    if summed[e] is None
                    else (summed[e].astype(F32) + got.astype(F32)).astype(BF16)
                )
        v.dkv_got = summed[0]

    def attend_near():
        v.dq, v.dkv = attend_back(
            place, doc_ends, queries, v.out_grads, near, v.dq_far, nz, ring, 0, 1, F32
        )

    def head_grads():
        cosine, signed = rope_tables(token_index - begin)
        v.grads = finish_grads(v.dq, v.dkv, v.dkv_got, cosine, signed)
        v.own_grads = [v.grads[0]] + [
            seq_swap(v.grads[d], d * ring) for d in range(1, nz)
        ]

    def turn_branch():
        v.branch_turned = turn(order, group, v.branch + v.branch_sib, spots)

    def grad_out():
        v.sent_out, v.part_out = weight_grad([v.branch_turned], [v.heads_placed])

    def send_out():
        (sent,) = hold([v.sent_out])
        v.low_out = low_sums(sent, v.part_out)

    def merge_out():
        v.kept_out, v.high_out = merge(*v.low_out)

    def high_out():
        (sent,) = hold([v.high_out])
        v.come_out = seq_swap(sent, high)

    def sum_out():
        v.own_out, sent = final_sum([v.kept_out, v.come_out])
        v.pair_out = seq_swap(sent, pair)

    def turn_rows():
        v.all_turned = turn_all(
            order, group, normed, [v.rows, v.rows_core[0], v.rows_x, v.rows_core[1]], m
        )

    def grad_qkv():
        v.sent_qkv, v.part_qkv = weight_grad(
            [v.all_turned], [jnp.concatenate(v.grads, axis=0)]
        )

    def send_qkv():
        (sent,) = hold([v.sent_qkv])
        v.low_qkv = low_sums(sent, v.part_qkv)

    def split_qkv():
        own, *sent = split_sum(*v.low_qkv, nz)
        v.qkv_heads = [own] + [seq_swap(sent[d - 1], d * ring) for d in range(1, nz)]

    def lay_qkv():
        v.shares = place_heads(place, v.qkv_heads)

    def rows_in():
        sib, v.in_mine = heads_project(place, v.own_grads, weights, nt, False)
        v.in_sib = mp_swap(sib, 1)

    def in_sum():
        v.in_parts = row_sum(v.in_mine, v.in_sib, CHUNKS)
        v.in_across = [mp_swap(part, 2) for part in v.in_parts]

    def norm_in_chunk(i):
        v.grad_rows[i], v.gain_attn[i] = norm_back(
            v.in_parts[i], v.in_across[i], x_chunks[i], v.residual_grad[i], gain_attn_row, (BF16,)
        )
        v.grad_sib[i] = mp_swap(v.grad_rows[i], 1)

    def join_in():
        v.input_grad = join_rows(place, v.grad_rows, v.grad_sib)

    def down_rows():
        v.down_mine, v.down_theirs = down(place, v.act, v.act_sib, w_down, v.down_sib, 2)

    def pair_rows():
        (sent,) = hold([v.down_theirs])
        v.down_got = seq_swap(sent, pair)

    def sum_rows():
        (v.down_part,) = row_sum(v.down_mine, v.down_got, 1)
        v.down_across = mp_swap(v.down_part, 2)

    def add_out():
        v.out_rows = add_rows(
            v.down_part, v.down_across, jnp.concatenate(v.residual, axis=0)
        )
        v.out_sib = mp_swap(v.out_rows, 1)

    def join_out():
        v.mixed_out = join_rows(place, [v.out_rows], [v.out_sib])

    def gains_core():
        (v.gains,) = hold([jnp.concatenate([sum(v.gain_attn), sum(v.gain_mlp)])])
        v.gains = v.gains + mp_swap(v.gains, 1)

    def gains_seq(bit):
        (v.gains,) = hold([v.gains])
        v.gains = v.gains + seq_swap(v.gains, 1 << bit)

    heads_out()
    dact_own()
    out_sum()
    swap_weights()
    norm_chunk(1)
    dact_sib()
    norm_chunk(0)
    turn_cot()
    hidden_sib()
    gather_z(2)
    gather_z(1)
    swap_cot()
    swap_dg()
    swap_du()
    turn_normed()
    swap_normed()
    hidden_own()
    grad_down()
    hidden_in()
    send_down()
    gather_z(3)
    grad_gate()
    back_chunk(1)
    send_gate()
    back_chunk(0)
    norm_back_chunk(1)
    norm_back_chunk(0)
    gather_x()
    heads_in()
    merge_down()
    high_down()
    grad_up()
    turn_branch()
    attend_far()
    gather_core()
    send_up()
    attend_near()
    merge_gate()
    high_gate()
    sum_down()
    head_grads()
    pair_down()
    rows_in()
    grad_out()
    merge_up()
    high_up()
    in_sum()
    down_rows()
    send_out()
    norm_in_chunk(0)
    turn_rows()
    grad_qkv()
    lay_down()
    merge_out()
    high_out()
    norm_in_chunk(1)
    pair_rows()
    send_qkv()
    sum_gate()
    join_in()
    gains_core()
    gains_seq(0)
    pair_gate()
    split_qkv()
    sum_up()
    pair_up()
    sum_rows()
    lay_up()
    gains_seq(2)
    sum_out()
    add_out()
    lay_gate()
    join_out()
    gains_seq(1)
    lay_qkv()
    for bit in range(3, bits):
        gains_seq(bit)
    gains = lax.dynamic_slice_in_dim(v.gains, s * group, group, 1)

    return (
        v.mixed_out,
        v.input_grad,
        *v.shares,
        (v.own_out + v.pair_out.astype(F32)).T,
        gains[0],
        v.gate_share,
        v.up_share,
        v.down_share,
        gains[1],
    )


def solution(mesh):
    placed = (
        P("seq", None),
        P(None, "mp"),
        P(None, "mp"),
        P(None, "mp"),
        P("mp", None),
        P(),
        P(None, "mp"),
        P(None, "mp"),
        P("mp", None),
        P(),
        P(),
        P("seq", None),
    )
    return jax.shard_map(
        functools.partial(layer, mesh.shape["seq"], mesh.shape["mp"]),
        mesh=mesh,
        in_specs=placed,
        out_specs=(
            P("seq", None),
            P("seq", None),
            P("seq", "mp"),
            P("seq", "mp"),
            P("seq", "mp"),
            P("mp", "seq"),
            P("seq"),
            P("seq", "mp"),
            P("seq", "mp"),
            P("mp", "seq"),
            P("seq"),
        ),
        check_vma=False,
    )
```

profile of v0, /device:TPU:0, one launch (start us, length us, event | category | flops | bytes accessed | tf_op | source)
XLA Modules:
  0.0 566.3 jit_solution(10103848567727309893)
XLA Ops:
  5.3 8.7 %project_qkv.2 = (bf16[512,384]{1,0:T(8,128)(2,1)}, bf16[512,384]{1,0:T(8,128)(2,1)}, bf16[512,2048]{1,0:T(8,128)(2,1)}) custom-call(s32[4]{0:T(128)} %pad_add_fusion.refs_0_, bf16[512,2048]{1,0:T(8,128)(2,1)} %refs_1_.4, f32[1,2048]{1,0:T(1,128)} %bitcast.41, bf16[2048,512]{1,0:T(8,128)(2,1)} %refs_5_.13, bf16[2048,512]{1,0:T(8,128)(2,1)} %refs_6_.3, ...), custom_call_target="tpu_custom_call" | custom-call | flops 3221225472 | bytes 16252928 | tf_op jit(solution)/shard_map/project_qkv/pallas_call | solution.py:67
  14.0 4.0 collective-permute-start.1
  18.0 7.3 %project_qkv.3 = (bf16[512,384]{1,0:T(8,128)(2,1)}, bf16[512,384]{1,0:T(8,128)(2,1)}) custom-call(s32[4]{0:T(128)} %pad_add_fusion.refs_0_, bf16[512,2048]{1,0:T(8,128)(2,1)} %get-tuple-element.160.refs_1_.refs_2_, bf16[2048,512]{1,0:T(8,128)(2,1)} %refs_5_.13, bf16[2048,512]{1,0:T(8,128)(2,1)} %refs_6_.3, bf16[2048,512]{1,0:T(8,128)(2,1)} %refs_7_.3, ...), custom_call_target="tpu_custom_call" | custom-call | flops 3221225472 | bytes 16252928 | tf_op jit(solution)/shard_map/project_qkv/pallas_call | solution.py:67
  30.3 4.8 constant_dynamic-slice_fusion.7
  35.2 7.7 %constant_dynamic-slice_fusion.5 = (bf16[2048,1024]{1,0:T(8,128)(2,1)}, bf16[2048,1024]{1,0:T(8,128)(2,1)}) fusion(bf16[2048,2048]{1,0:T(8,128)(2,1)} %refs_7_.2, s32[]{:T(128)S(6)} %select_n.39, bf16[2048,2048]{1,0:T(8,128)(2,1)} %refs_5_.11), kind=kLoop, calls=%fused_computation.22 | loop fusion | bytes 16777220 | tf_op jit(solution)/shard_map/dynamic_slice | solution.py:1206
  42.9 8.9 %collective-permute-done.refs_3_.refs_7_.refs_11_ = bf16[512,384]{1,0:T(8,128)(2,1)S(1)} collective-permute-done((bf16[512,384]{1,0:T(8,128)(2,1)}, bf16[512,384]{1,0:T(8,128)(2,1)S(1)}, u32[]{:S(2)}, u32[]{:S(2)}) %collective-permute-start) | collective-permute-done | bytes 393248 | tf_op jit(solution)/shard_map/ppermute | solution.py:1154
  55.9 5.2 collective-permute-done.4.refs_11_
  61.1 5.6 collective-permute-done.5.refs_12_
  66.7 3.9 collective-permute-done.6.refs_13_
  70.7 15.8 %attend.1 = (bf16[512,128]{1,0:T(8,128)(2,1)S(1)}, bf16[512,128]{1,0:T(8,128)(2,1)S(1)}, bf16[512,128]{1,0:T(8,128)(2,1)S(1)}, bf16[512,128]{1,0:T(8,128)(2,1)S(1)}) custom-call(s32[4]{0:T(128)S(1)} %copy-done.59, s32[5]{0:T(128)S(1)} %copy-done.64, bf16[512,384]{1,0:T(8,128)(2,1)S(1)} %copy-done.51, ...), custom_call_target="tpu_custom_call" | custom-call | flops 8589934592 | bytes 6291456 | tf_op jit(solution)/shard_map/attend/pallas_call | solution.py:67
  92.0 6.5 %collective-permute-done.8.refs_3_ = bf16[512,128]{1,0:T(8,128)(2,1)S(1)} collective-permute-done((bf16[512,128]{1,0:T(8,128)(2,1)S(1)}, bf16[512,128]{1,0:T(8,128)(2,1)S(1)}, u32[]{:S(2)}, u32[]{:S(2)}) %collective-permute-start.8) | collective-permute-done | bytes 131104 | tf_op jit(solution)/shard_map/ppermute | solution.py:1154
  102.4 6.2 %hidden_upstream.2.refs_2_.refs_7_ = bf16[512,1024]{1,0:T(8,128)(2,1)} custom-call(s32[4]{0:T(128)S(1)} %copy-done.59, bf16[128,2048]{1,0:T(8,128)(2,1)S(1)} %get-tuple-element.336.refs_1_.refs_2_.refs_3_, bf16[128,2048]{1,0:T(8,128)(2,1)S(1)} %get-tuple-element.335.refs_2_.refs_3_, bf16[128,2048]{1,0:T(8,128)(2,1)S(1)} %get-tuple-element.334.refs_3_.refs_4_, ...), custom_call_target="tpu_custom_call" | custom-call | flops 4294967296 | bytes 16777216 | tf_op jit(solution)/shard_map/hidden_upstream/pallas_call | solution.py:67
  115.1 11.8 %collective-permute-done.14.refs_1_ = bf16[128,2048]{1,0:T(8,128)(2,1)} collective-permute-done((bf16[128,2048]{1,0:T(8,128)(2,1)}, bf16[128,2048]{1,0:T(8,128)(2,1)}, u32[]{:S(2)}, u32[]{:S(2)}) %collective-permute-start.14) | collective-permute-done | bytes 524320 | tf_op jit(solution)/shard_map/ppermute | solution.py:1157
  131.4 5.7 %hidden_upstream.3.refs_4_.refs_7_ = bf16[512,1024]{1,0:T(8,128)(2,1)} custom-call(s32[4]{0:T(128)S(1)} %copy-done.59, bf16[128,2048]{1,0:T(8,128)(2,1)S(1)} %get-tuple-element.336.refs_1_.refs_2_.refs_3_, bf16[128,2048]{1,0:T(8,128)(2,1)S(1)} %get-tuple-element.335.refs_2_.refs_3_, bf16[128,2048]{1,0:T(8,128)(2,1)S(1)} %get-tuple-element.334.refs_3_.refs_4_, ...), custom_call_target="tpu_custom_call" | custom-call | flops 4294967296 | bytes 16777216 | tf_op jit(solution)/shard_map/hidden_upstream/pallas_call | solution.py:67
  147.0 6.2 %collective-permute-done.15.refs_3_.refs_4_ = bf16[128,2048]{1,0:T(8,128)(2,1)S(1)} collective-permute-done((bf16[128,2048]{1,0:T(8,128)(2,1)S(1)}, bf16[128,2048]{1,0:T(8,128)(2,1)S(1)}, u32[]{:S(2)}, u32[]{:S(2)}) %collective-permute-start.15) | collective-permute-done | bytes 524320 | tf_op jit(solution)/shard_map/ppermute | solution.py:1154
  153.2 10.1 %hidden.2 = (bf16[512,1024]{1,0:T(8,128)(2,1)}, bf16[512,1024]{1,0:T(8,128)(2,1)}, bf16[512,1024]{1,0:T(8,128)(2,1)}) custom-call(s32[4]{0:T(128)S(1)} %copy-done.59, bf16[128,2048]{1,0:T(8,128)(2,1)S(1)} %get-tuple-element.181.refs_1_.refs_2_, bf16[128,2048]{1,0:T(8,128)(2,1)S(1)} %get-tuple-element.182.refs_2_.refs_3_, ...), custom_call_target="tpu_custom_call" | custom-call | flops 8589934592 | bytes 29360128 | tf_op jit(solution)/shard_map/hidden/pallas_call | solution.py:67
  170.1 10.1 %hidden.3 = (bf16[512,1024]{1,0:T(8,128)(2,1)}, bf16[512,1024]{1,0:T(8,128)(2,1)}, bf16[512,1024]{1,0:T(8,128)(2,1)}) custom-call(s32[4]{0:T(128)S(1)} %copy-done.59, bf16[128,2048]{1,0:T(8,128)(2,1)S(1)} %get-tuple-element.181.refs_1_.refs_2_, bf16[128,2048]{1,0:T(8,128)(2,1)S(1)} %get-tuple-element.182.refs_2_.refs_3_, ...), custom_call_target="tpu_custom_call" | custom-call | flops 8589934592 | bytes 29360128 | tf_op jit(solution)/shard_map/hidden/pallas_call | solution.py:67
  181.4 8.6 %weight_grad.5 = (bf16[1024,1024]{1,0:T(8,128)(2,1)}, bf16[1024,1024]{1,0:T(8,128)(2,1)}) custom-call(bf16[2048,512]{1,0:T(8,128)(2,1)} %copy-done.28, bf16[2048,512]{1,0:T(8,128)(2,1)} %collective-permute-done.19.refs_1_, bf16[512,1024]{1,0:T(8,128)(2,1)S(1)} %copy-done.85, bf16[512,1024]{1,0:T(8,128)(2,1)} %collective-permute-done.20.refs_3_, ...), custom_call_target="tpu_custom_call" | custom-call | flops 8589934592 | bytes 20971520 | tf_op jit(solution)/shard_map/weight_grad/pallas_call | solution.py:67
  190.0 15.8 %hidden_back.1 = (bf16[128,2048]{1,0:T(8,128)(2,1)S(1)}, bf16[128,2048]{1,0:T(8,128)(2,1)S(1)}, bf16[128,2048]{1,0:T(8,128)(2,1)S(1)}, bf16[128,2048]{1,0:T(8,128)(2,1)}) custom-call(s32[4]{0:T(128)S(1)} %copy-done.59, bf16[512,1024]{1,0:T(8,128)(2,1)} %get-tuple-element.196.refs_1_.refs_2_, bf16[512,1024]{1,0:T(8,128)(2,1)} %get-tuple-element.203.refs_2_, ...), custom_call_target="tpu_custom_call" | custom-call | flops 17179869184 | bytes 46137344 | tf_op jit(solution)/shard_map/hidden_back/pallas_call | solution.py:67
  207.9 4.9 collective-permute-start.36
  214.1 8.6 %weight_grad.6 = (bf16[1024,1024]{1,0:T(8,128)(2,1)}, bf16[1024,1024]{1,0:T(8,128)(2,1)}) custom-call(bf16[2048,512]{1,0:T(8,128)(2,1)} %copy-done.21, bf16[2048,512]{1,0:T(8,128)(2,1)} %copy-done.97, bf16[512,1024]{1,0:T(8,128)(2,1)S(1)} %copy-done.87, bf16[512,1024]{1,0:T(8,128)(2,1)} %collective-permute-done.23.refs_3_, ...), custom_call_target="tpu_custom_call" | custom-call | flops 8589934592 | bytes 20971520 | tf_op jit(solution)/shard_map/weight_grad/pallas_call | solution.py:67
  226.1 5.1 collective-permute-done.21.refs_1_
  233.7 5.9 %collective-permute-done.27.refs_1_ = bf16[128,2048]{1,0:T(8,128)(2,1)} collective-permute-done((bf16[128,2048]{1,0:T(8,128)(2,1)S(1)}, bf16[128,2048]{1,0:T(8,128)(2,1)}, u32[]{:S(2)}, u32[]{:S(2)}) %collective-permute-start.27) | collective-permute-done | bytes 524320 | tf_op jit(solution)/shard_map/ppermute | solution.py:1157
  244.5 4.4 collective-permute-done.26.refs_1_
  252.1 5.8 %fusion = (f32[4,512,64]{2,1,0:T(8,128)}, f32[4,512,64]{2,1,0:T(8,128)}, f32[4,512,64]{2,1,0:T(8,128)}) fusion(f32[64]{0:T(128)S(1)} %copy-done.96, f32[4,512]{1,0:T(4,128)S(1)} %subtract_convert_fusion), kind=kLoop, calls=%fused_computation.9 | loop fusion | flops 262144 | bytes 1581312 | tf_op jit(solution)/shard_map/neg | solution.py:1110
  267.1 4.1 collective-permute-start.40
  271.2 3.9 merge.4
  279.0 8.6 %weight_grad.7 = (bf16[1024,1024]{1,0:T(8,128)(2,1)}, bf16[1024,1024]{1,0:T(8,128)(2,1)}) custom-call(bf16[2048,512]{1,0:T(8,128)(2,1)} %copy-done.21, bf16[2048,512]{1,0:T(8,128)(2,1)} %copy-done.97, bf16[512,1024]{1,0:T(8,128)(2,1)S(1)} %copy-done.86, bf16[512,1024]{1,0:T(8,128)(2,1)} %collective-permute-done.35.refs_3_, f32[512,1024]{1,0:T(8,128)} %copy-done.26), custom_call_target="tpu_custom_call" | custom-call | flops 8589934592 | bytes 20971520 | tf_op jit(solution)/shard_map/weight_grad/pallas_call | solution.py:67
  289.7 8.2 %attend_back.2 = (f32[4,512,128]{2,1,0:T(8,128)S(1)}, bf16[4,512,256]{2,1,0:T(8,128)(2,1)S(1)}) custom-call(s32[4]{0:T(128)S(1)} %copy-done.59, s32[5]{0:T(128)S(1)} %copy-done.65, bf16[512,384]{1,0:T(8,128)(2,1)S(1)} %copy-done.52, bf16[512,384]{1,0:T(8,128)(2,1)S(1)} %copy-done.54, bf16[512,384]{1,0:T(8,128)(2,1)S(1)} %collective-permute-done.1.refs_4_.refs_8_.refs_12_, ...), custom_call_target="tpu_custom_call" | custom-call | flops 10737418240 | bytes 6291456 | tf_op jit(solution)/shard_map/attend_back/pallas_call | solution.py:67
  297.9 7.4 %collective-permute-start.38 = (bf16[4,512,256]{2,1,0:T(8,128)(2,1)S(1)}, bf16[4,512,256]{2,1,0:T(8,128)(2,1)S(1)}, u32[]{:S(2)}, u32[]{:S(2)}) collective-permute-start(bf16[4,512,256]{2,1,0:T(8,128)(2,1)S(1)} %get-tuple-element.233), channel_id=1, source_target_pairs={{0,4},{4,0},{8,12},{12,8},{16,20},{20,16},{24,28},{28,24},{1,5},{5... | collective-permute-start | bytes 3145736 | tf_op jit(solution)/shard_map/ppermute | solution.py:1154
  305.9 3.9 collective-permute-done.37.refs_5_
  310.2 13.1 %attend_back.3 = (f32[4,512,128]{2,1,0:T(8,128)S(1)}, f32[4,512,256]{2,1,0:T(8,128)S(1)}) custom-call(s32[4]{0:T(128)S(1)} %copy-done.59, s32[5]{0:T(128)S(1)} %copy-done.65, bf16[512,384]{1,0:T(8,128)(2,1)S(1)} %copy-done.52, bf16[512,384]{1,0:T(8,128)(2,1)S(1)} %copy-done.54, bf16[512,384]{1,0:T(8,128)(2,1)S(1)} %collective-permute-done.1.refs_4_.refs_8_.refs_12_, ...), custom_call_target="tpu_custom_call" | custom-call | flops 10737418240 | bytes 6291456 | tf_op jit(solution)/shard_map/attend_back/pallas_call | solution.py:67
  323.4 3.9 merge.5
  328.4 11.9 %collective-permute-done.38.refs_2_ = bf16[4,512,256]{2,1,0:T(8,128)(2,1)S(1)} collective-permute-done((bf16[4,512,256]{2,1,0:T(8,128)(2,1)S(1)}, bf16[4,512,256]{2,1,0:T(8,128)(2,1)S(1)}, u32[]{:S(2)}, u32[]{:S(2)}) %collective-permute-start.38) | collective-permute-done | bytes 1048608 | tf_op jit(solution)/shard_map/ppermute | solution.py:1154
  346.1 10.5 %collective-permute-done.41.refs_2_ = bf16[512,384]{1,0:T(8,128)(2,1)S(1)} collective-permute-done((bf16[512,384]{1,0:T(8,128)(2,1)}, bf16[512,384]{1,0:T(8,128)(2,1)S(1)}, u32[]{:S(2)}, u32[]{:S(2)}) %collective-permute-start.41) | collective-permute-done | bytes 393248 | tf_op jit(solution)/shard_map/ppermute | solution.py:1154
  356.6 11.7 %collective-permute-done.42.refs_3_ = bf16[512,384]{1,0:T(8,128)(2,1)S(1)} collective-permute-done((bf16[512,384]{1,0:T(8,128)(2,1)}, bf16[512,384]{1,0:T(8,128)(2,1)S(1)}, u32[]{:S(2)}, u32[]{:S(2)}) %collective-permute-start.42) | collective-permute-done | bytes 393248 | tf_op jit(solution)/shard_map/ppermute | solution.py:1154
  368.3 4.4 heads_project.3
  373.2 5.7 %collective-permute-start.55 = (bf16[512,1024]{1,0:T(8,128)(2,1)}, bf16[512,1024]{1,0:T(8,128)(2,1)}, u32[]{:S(2)}, u32[]{:S(2)}) collective-permute-start(bf16[512,1024]{1,0:T(8,128)(2,1)} %get-tuple-element.277), channel_id=1, source_target_pairs={{0,16},{4,20},{8,24},{12,28},{16,0},{20,4},{24,8},{28,12},{1,17},{... | collective-permute-start | bytes 3145736 | tf_op jit(solution)/shard_map/ppermute | solution.py:1154
  380.0 4.4 weight_grad.8
  386.4 3.9 merge.6
  394.6 9.2 %down.1 = (bf16[256,2048]{1,0:T(8,128)(2,1)S(1)}, bf16[256,2048]{1,0:T(8,128)(2,1)}) custom-call(s32[4]{0:T(128)S(1)} %copy-done.59, bf16[512,1024]{1,0:T(8,128)(2,1)} %get-tuple-element.195.refs_2_.refs_4_.refs_1_, bf16[512,1024]{1,0:T(8,128)(2,1)} %get-tuple-element.193.refs_6_.refs_2_, bf16[2048,2048]{1,0:T(8,128)(2,1)} %refs_3_.5, ...), custom_call_target="tpu_custom_call" | custom-call | flops 8589934592 | bytes 25165824 | tf_op jit(solution)/shard_map/down/pallas_call | solution.py:67
  413.5 10.0 %turn_all.1.refs_0_.refs_2_ = bf16[2048,2048]{1,0:T(8,128)(2,1)} custom-call(s32[1]{0:T(128)} %bitcast.2.refs_0_, s32[8]{0:T(128)S(1)} %broadcast_xor_fusion.refs_1_, bf16[512,2048]{1,0:T(8,128)(2,1)} %get-tuple-element.160.refs_1_.refs_2_, bf16[3,128,2048]{2,1,0:T(8,128)(2,1)} %copy-done.7, bf16[3,128,2048]{2,1,0:T(8,128)(2,1)} %collective-permute-done.49.refs_4_, ...), custom_call_target="tpu_custom_call" | custom-call | flops 4294967296 | bytes 33554432 | tf_op jit(solution)/shard_map/turn_all/pallas_call | solution.py:67
  423.5 7.6 %weight_grad.9 = (bf16[1024,384]{1,0:T(8,128)(2,1)S(1)}, bf16[1024,384]{1,0:T(8,128)(2,1)S(1)}) custom-call(bf16[2048,2048]{1,0:T(8,128)(2,1)} %turn_all.1.refs_0_.refs_2_, bf16[2048,384]{1,0:T(8,128)(2,1)} %pad_maximum_fusion.1.refs_1_, bf16[2048,2048]{1,0:T(8,128)(2,1)} %turn_all.1.refs_0_.refs_2_), custom_call_target="tpu_custom_call" | custom-call | flops 6442450944 | bytes 23068672 | tf_op jit(solution)/shard_map/weight_grad/pallas_call | solution.py:67
  453.9 10.2 %collective-permute-done.54.refs_1_ = bf16[1024,384]{1,0:T(8,128)(2,1)S(1)} collective-permute-done((bf16[1024,384]{1,0:T(8,128)(2,1)S(1)}, bf16[1024,384]{1,0:T(8,128)(2,1)S(1)}, u32[]{:S(2)}, u32[]{:S(2)}) %collective-permute-start.54) | collective-permute-done | bytes 786464 | tf_op jit(solution)/shard_map/ppermute | solution.py:1154
  465.8 4.7 collective-permute-done.53
  472.0 20.8 %collective-permute-done.52.refs_1_ = bf16[256,2048]{1,0:T(8,128)(2,1)S(1)} collective-permute-done((bf16[256,2048]{1,0:T(8,128)(2,1)S(1)}, bf16[256,2048]{1,0:T(8,128)(2,1)S(1)}, u32[]{:S(2)}, u32[]{:S(2)}) %collective-permute-start.52) | collective-permute-done | bytes 1048608 | tf_op jit(solution)/shard_map/ppermute | solution.py:1154
  501.7 17.3 %collective-permute-done.62.refs_2_ = bf16[256,1024]{1,0:T(8,128)(2,1)S(1)} collective-permute-done((bf16[256,1024]{1,0:T(8,128)(2,1)S(1)}, bf16[256,1024]{1,0:T(8,128)(2,1)S(1)}, u32[]{:S(2)}, u32[]{:S(2)}) %collective-permute-start.62) | collective-permute-done | bytes 524320 | tf_op jit(solution)/shard_map/ppermute | solution.py:1154
  528.8 13.7 %collective-permute-done.68 = f32[2,2048]{1,0:T(2,128)} collective-permute-done((f32[2,2048]{1,0:T(2,128)}, f32[2,2048]{1,0:T(2,128)}, u32[]{:S(2)}, u32[]{:S(2)}) %collective-permute-start.68) | collective-permute-done | bytes 16416 | tf_op jit(solution)/shard_map/ppermute | solution.py:1154
  (385 shorter events, 177.2 us)
Async XLA Ops:
  14.0 39.5 %collective-permute-start.1 = (bf16[512,384]{1,0:T(8,128)(2,1)}, bf16[512,384]{1,0:T(8,128)(2,1)S(1)}, u32[]{:S(2)}, u32[]{:S(2)}) collective-permute-start(bf16[512,384]{1,0:T(8,128)(2,1)} %get-tuple-element.161.refs_7_), channel_id=1, source_target_pairs={{0,16},{4,20},{8,24},{12,28},{16,0},{20,4},{24,8},{28,12},{1,17},{... | collective-permute-start | bytes 1179656 | tf_op jit(solution)/shard_map/ppermute | solution.py:1154
  25.3 26.4 %collective-permute-start = (bf16[512,384]{1,0:T(8,128)(2,1)}, bf16[512,384]{1,0:T(8,128)(2,1)S(1)}, u32[]{:S(2)}, u32[]{:S(2)}) collective-permute-start(bf16[512,384]{1,0:T(8,128)(2,1)} %get-tuple-element.163), channel_id=1, source_target_pairs={{0,8},{4,12},{8,0},{12,4},{16,24},{20,28},{24,16},{28,20},{1,9},{5... | collective-permute-start | bytes 1179656 | tf_op jit(solution)/shard_map/ppermute | solution.py:1154
  26.9 27.1 %collective-permute-start.2 = (bf16[512,384]{1,0:T(8,128)(2,1)}, bf16[512,384]{1,0:T(8,128)(2,1)S(1)}, u32[]{:S(2)}, u32[]{:S(2)}) collective-permute-start(bf16[512,384]{1,0:T(8,128)(2,1)} %get-tuple-element.164), channel_id=1, source_target_pairs={{0,24},{4,28},{8,16},{12,20},{16,8},{20,12},{24,0},{28,4},{1,25},{... | collective-permute-start | bytes 1179656 | tf_op jit(solution)/shard_map/ppermute | solution.py:1154
  28.6 27.3 %collective-permute-start.3 = (bf16[512,256]{1,0:T(8,128)(2,1)}, bf16[512,256]{1,0:T(8,128)(2,1)S(1)}, u32[]{:S(2)}, u32[]{:S(2)}) collective-permute-start(bf16[512,256]{1,0:T(8,128)(2,1)} %slice.44), channel_id=1, source_target_pairs={{0,4},{4,0},{8,12},{12,8},{16,20},{20,16},{24,28},{28,24},{1,5},{5... | collective-permute-start | bytes 786440 | tf_op jit(solution)/shard_map/ppermute | solution.py:1154
  54.0 16.7 %collective-permute-start.6 = (bf16[512,256]{1,0:T(8,128)(2,1)S(1)}, bf16[512,256]{1,0:T(8,128)(2,1)S(1)}, u32[]{:S(2)}, u32[]{:S(2)}) collective-permute-start(bf16[512,256]{1,0:T(8,128)(2,1)S(1)} %slice.60), channel_id=1, source_target_pairs={{0,4},{4,0},{8,12},{12,8},{16,20},{20,16},{24,28},{28,24},{1,5},{5... | collective-permute-start | bytes 786440 | tf_op jit(solution)/shard_map/ppermute | solution.py:1154
  55.8 42.7 %collective-permute-start.10 = (bf16[256,2048]{1,0:T(8,128)(2,1)S(1)}, bf16[256,2048]{1,0:T(8,128)(2,1)S(1)}, u32[]{:S(2)}, u32[]{:S(2)}) collective-permute-start(bf16[256,2048]{1,0:T(8,128)(2,1)S(1)} %constant_dynamic-slice_fusion.8), channel_id=1, source_target_pairs={{0,8},{4,12},{8,0},{12,4},{16,24},{20,28},{24,16},{28,20},{1,9},{5... | collective-permute-start | bytes 3145736 | tf_op jit(solution)/shard_map/ppermute | solution.py:1154
  110.8 20.7 %collective-permute-start.13 = (bf16[1024,2048]{1,0:T(8,128)(2,1)}, bf16[1024,2048]{1,0:T(8,128)(2,1)}, u32[]{:S(2)}, u32[]{:S(2)}) collective-permute-start(bf16[1024,2048]{1,0:T(8,128)(2,1)} %constant_dynamic-slice_fusion.7), channel_id=1, source_target_pairs={{0,1},{1,0},{2,3},{3,2},{4,5},{5,4},{6,7},{7,6},{8,9},{9,8},{10,11... | collective-permute-start | bytes 12582920 | tf_op jit(solution)/shard_map/ppermute | solution.py:1157
  111.2 35.7 %collective-permute-start.17 = (bf16[2048,1024]{1,0:T(8,128)(2,1)}, bf16[2048,1024]{1,0:T(8,128)(2,1)}, u32[]{:S(2)}, u32[]{:S(2)}) collective-permute-start(bf16[2048,1024]{1,0:T(8,128)(2,1)} %get-tuple-element.183), channel_id=1, source_target_pairs={{0,1},{1,0},{2,3},{3,2},{4,5},{5,4},{6,7},{7,6},{8,9},{9,8},{10,11... | collective-permute-start | bytes 12582920 | tf_op jit(solution)/shard_map/ppermute | solution.py:1157
  111.3 35.7 %collective-permute-start.18 = (bf16[2048,1024]{1,0:T(8,128)(2,1)}, bf16[2048,1024]{1,0:T(8,128)(2,1)}, u32[]{:S(2)}, u32[]{:S(2)}) collective-permute-start(bf16[2048,1024]{1,0:T(8,128)(2,1)} %get-tuple-element.184), channel_id=1, source_target_pairs={{0,1},{1,0},{2,3},{3,2},{4,5},{5,4},{6,7},{7,6},{8,9},{9,8},{10,11... | collective-permute-start | bytes 12582920 | tf_op jit(solution)/shard_map/ppermute | solution.py:1157
  113.3 23.9 %collective-permute-start.12 = (bf16[128,2048]{1,0:T(8,128)(2,1)S(1)}, bf16[128,2048]{1,0:T(8,128)(2,1)}, u32[]{:S(2)}, u32[]{:S(2)}) collective-permute-start(bf16[128,2048]{1,0:T(8,128)(2,1)S(1)} %get-tuple-element.179.refs_4_.refs_0_), channel_id=1, source_target_pairs={{0,2},{1,3},{2,0},{3,1},{4,6},{5,7},{6,4},{7,5},{8,10},{9,11},{10,... | collective-permute-start | bytes 1572872 | tf_op jit(solution)/shard_map/ppermute | solution.py:1157
  129.5 17.5 %collective-permute-start.16 = (bf16[128,2048]{1,0:T(8,128)(2,1)S(1)}, bf16[128,2048]{1,0:T(8,128)(2,1)S(1)}, u32[]{:S(2)}, u32[]{:S(2)}) collective-permute-start(bf16[128,2048]{1,0:T(8,128)(2,1)S(1)} %get-tuple-element.182.refs_2_.refs_3_), channel_id=1, source_target_pairs={{0,8},{4,12},{8,0},{12,4},{16,24},{20,28},{24,16},{28,20},{1,9},{5... | collective-permute-start | bytes 1572872 | tf_op jit(solution)/shard_map/ppermute | solution.py:1154
  163.3 16.9 %collective-permute-start.19 = (bf16[2048,512]{1,0:T(8,128)(2,1)S(1)}, bf16[2048,512]{1,0:T(8,128)(2,1)}, u32[]{:S(2)}, u32[]{:S(2)}) collective-permute-start(bf16[2048,512]{1,0:T(8,128)(2,1)S(1)} %copy-done.29), channel_id=1, source_target_pairs={{0,1},{1,0},{2,3},{3,2},{4,5},{5,4},{6,7},{7,6},{8,9},{9,8},{10,11... | collective-permute-start | bytes 6291464 | tf_op jit(solution)/shard_map/ppermute | solution.py:1157
  163.3 16.9 %collective-permute-start.20 = (bf16[512,1024]{1,0:T(8,128)(2,1)}, bf16[512,1024]{1,0:T(8,128)(2,1)}, u32[]{:S(2)}, u32[]{:S(2)}) collective-permute-start(bf16[512,1024]{1,0:T(8,128)(2,1)} %get-tuple-element.193.refs_6_.refs_2_), channel_id=1, source_target_pairs={{0,1},{1,0},{2,3},{3,2},{4,5},{5,4},{6,7},{7,6},{8,9},{9,8},{10,11... | collective-permute-start | bytes 3145736 | tf_op jit(solution)/shard_map/ppermute | solution.py:1157
  167.9 37.9 %collective-permute-start.24 = (bf16[128,2048]{1,0:T(8,128)(2,1)}, bf16[128,2048]{1,0:T(8,128)(2,1)S(1)}, u32[]{:S(2)}, u32[]{:S(2)}) collective-permute-start(bf16[128,2048]{1,0:T(8,128)(2,1)} %constant_dynamic-slice_fusion.3), channel_id=1, source_target_pairs={{0,16},{4,20},{8,24},{12,28},{16,0},{20,4},{24,8},{28,12},{1,17},{... | collective-permute-start | bytes 1572872 | tf_op jit(solution)/shard_map/ppermute | solution.py:1154
  169.6 43.2 %collective-permute-start.22 = (bf16[2048,512]{1,0:T(8,128)(2,1)S(1)}, bf16[2048,512]{1,0:T(8,128)(2,1)S(1)}, u32[]{:S(2)}, u32[]{:S(2)}) collective-permute-start(bf16[2048,512]{1,0:T(8,128)(2,1)S(1)} %turn.4.refs_8_.refs_0_), channel_id=1, source_target_pairs={{0,1},{1,0},{2,3},{3,2},{4,5},{5,4},{6,7},{7,6},{8,9},{9,8},{10,11... | collective-permute-start | bytes 6291464 | tf_op jit(solution)/shard_map/ppermute | solution.py:1157
  169.6 43.2 %collective-permute-start.23 = (bf16[512,1024]{1,0:T(8,128)(2,1)}, bf16[512,1024]{1,0:T(8,128)(2,1)}, u32[]{:S(2)}, u32[]{:S(2)}) collective-permute-start(bf16[512,1024]{1,0:T(8,128)(2,1)} %get-tuple-element.203.refs_2_), channel_id=1, source_target_pairs={{0,1},{1,0},{2,3},{3,2},{4,5},{5,4},{6,7},{7,6},{8,9},{9,8},{10,11... | collective-permute-start | bytes 3145736 | tf_op jit(solution)/shard_map/ppermute | solution.py:1157
  205.8 17.0 %collective-permute-start.25 = (bf16[128,2048]{1,0:T(8,128)(2,1)}, bf16[128,2048]{1,0:T(8,128)(2,1)S(1)}, u32[]{:S(2)}, u32[]{:S(2)}) collective-permute-start(bf16[128,2048]{1,0:T(8,128)(2,1)} %get-tuple-element.209), channel_id=1, source_target_pairs={{0,8},{4,12},{8,0},{12,4},{16,24},{20,28},{24,16},{28,20},{1,9},{5... | collective-permute-start | bytes 1572872 | tf_op jit(solution)/shard_map/ppermute | solution.py:1154
  206.6 24.6 %collective-permute-start.21 = (bf16[128,2048]{1,0:T(8,128)(2,1)S(1)}, bf16[128,2048]{1,0:T(8,128)(2,1)S(1)}, u32[]{:S(2)}, u32[]{:S(2)}) collective-permute-start(bf16[128,2048]{1,0:T(8,128)(2,1)S(1)} %get-tuple-element.201), channel_id=1, source_target_pairs={{0,8},{4,12},{8,0},{12,4},{16,24},{20,28},{24,16},{28,20},{1,9},{5... | collective-permute-start | bytes 1572872 | tf_op jit(solution)/shard_map/ppermute | solution.py:1154
  207.9 59.2 %collective-permute-start.36 = (bf16[1024,1024]{1,0:T(8,128)(2,1)}, bf16[1024,1024]{1,0:T(8,128)(2,1)}, u32[]{:S(2)}, u32[]{:S(2)}) collective-permute-start(bf16[1024,1024]{1,0:T(8,128)(2,1)} %get-tuple-element.223.refs_9_), channel_id=1, source_target_pairs={{0,4},{4,0},{8,12},{12,8},{16,20},{20,16},{24,28},{28,24},{1,5},{5... | collective-permute-start | bytes 6291464 | tf_op jit(solution)/shard_map/ppermute | solution.py:1154
  231.3 17.6 %collective-permute-start.26 = (bf16[128,2048]{1,0:T(8,128)(2,1)S(1)}, bf16[128,2048]{1,0:T(8,128)(2,1)}, u32[]{:S(2)}, u32[]{:S(2)}) collective-permute-start(bf16[128,2048]{1,0:T(8,128)(2,1)S(1)} %row_sum.7.refs_5_.refs_0_), channel_id=1, source_target_pairs={{0,2},{1,3},{2,0},{3,1},{4,6},{5,7},{6,4},{7,5},{8,10},{9,11},{10,... | collective-permute-start | bytes 1572872 | tf_op jit(solution)/shard_map/ppermute | solution.py:1157
  232.9 18.6 %collective-permute-start.30 = (bf16[128,2048]{1,0:T(8,128)(2,1)}, bf16[128,2048]{1,0:T(8,128)(2,1)}, u32[]{:S(2)}, u32[]{:S(2)}) collective-permute-start(bf16[128,2048]{1,0:T(8,128)(2,1)} %constant_dynamic-slice_fusion.3), channel_id=1, source_target_pairs={{0,8},{4,12},{8,0},{12,4},{16,24},{20,28},{24,16},{28,20},{1,9},{5... | collective-permute-start | bytes 1572872 | tf_op jit(solution)/shard_map/ppermute | solution.py:1154
  233.7 45.4 %collective-permute-start.35 = (bf16[512,1024]{1,0:T(8,128)(2,1)}, bf16[512,1024]{1,0:T(8,128)(2,1)}, u32[]{:S(2)}, u32[]{:S(2)}) collective-permute-start(bf16[512,1024]{1,0:T(8,128)(2,1)} %get-tuple-element.221.refs_4_), channel_id=1, source_target_pairs={{0,1},{1,0},{2,3},{3,2},{4,5},{5,4},{6,7},{7,6},{8,9},{9,8},{10,11... | collective-permute-start | bytes 3145736 | tf_op jit(solution)/shard_map/ppermute | solution.py:1157
  239.6 18.3 %collective-permute-start.31 = (bf16[128,2048]{1,0:T(8,128)(2,1)}, bf16[128,2048]{1,0:T(8,128)(2,1)S(1)}, u32[]{:S(2)}, u32[]{:S(2)}) collective-permute-start(bf16[128,2048]{1,0:T(8,128)(2,1)} %copy-done.46), channel_id=1, source_target_pairs={{0,8},{4,12},{8,0},{12,4},{16,24},{20,28},{24,16},{28,20},{1,9},{5... | collective-permute-start | bytes 1572872 | tf_op jit(solution)/shard_map/ppermute | solution.py:1154
  267.1 56.3 %collective-permute-start.40 = (bf16[1024,1024]{1,0:T(8,128)(2,1)S(1)}, bf16[1024,1024]{1,0:T(8,128)(2,1)}, u32[]{:S(2)}, u32[]{:S(2)}) collective-permute-start(bf16[1024,1024]{1,0:T(8,128)(2,1)S(1)} %copy-done.20), channel_id=1, source_target_pairs={{0,4},{4,0},{8,12},{12,8},{16,20},{20,16},{24,28},{28,24},{1,5},{5... | collective-permute-start | bytes 6291464 | tf_op jit(solution)/shard_map/ppermute | solution.py:1154
  276.4 33.4 %collective-permute-start.37 = (bf16[3,128,2048]{2,1,0:T(8,128)(2,1)S(1)}, bf16[3,128,2048]{2,1,0:T(8,128)(2,1)}, u32[]{:S(2)}, u32[]{:S(2)}) collective-permute-start(bf16[3,128,2048]{2,1,0:T(8,128)(2,1)S(1)} %stack_rows.1.refs_6_.refs_3_), channel_id=1, source_target_pairs={{0,2},{1,3},{2,0},{3,1},{4,6},{5,7},{6,4},{7,5},{8,10},{9,11},{10,... | collective-permute-start | bytes 4718600 | tf_op jit(solution)/shard_map/ppermute | solution.py:1157
  277.0 50.3 %collective-permute-start.39 = (bf16[512,1024]{1,0:T(8,128)(2,1)}, bf16[512,1024]{1,0:T(8,128)(2,1)S(1)}, u32[]{:S(2)}, u32[]{:S(2)}) collective-permute-start(bf16[512,1024]{1,0:T(8,128)(2,1)} %get-tuple-element.234), channel_id=1, source_target_pairs={{0,16},{4,20},{8,24},{12,28},{16,0},{20,4},{24,8},{28,12},{1,17},{... | collective-permute-start | bytes 3145736 | tf_op jit(solution)/shard_map/ppermute | solution.py:1154
  297.9 42.3 %collective-permute-start.38 = (bf16[4,512,256]{2,1,0:T(8,128)(2,1)S(1)}, bf16[4,512,256]{2,1,0:T(8,128)(2,1)S(1)}, u32[]{:S(2)}, u32[]{:S(2)}) collective-permute-start(bf16[4,512,256]{2,1,0:T(8,128)(2,1)S(1)} %get-tuple-element.233), channel_id=1, source_target_pairs={{0,4},{4,0},{8,12},{12,8},{16,20},{20,16},{24,28},{28,24},{1,5},{5... | collective-permute-start | bytes 3145736 | tf_op jit(solution)/shard_map/ppermute | solution.py:1154
  309.9 74.5 %collective-permute-start.45 = (bf16[1024,1024]{1,0:T(8,128)(2,1)}, bf16[1024,1024]{1,0:T(8,128)(2,1)}, u32[]{:S(2)}, u32[]{:S(2)}) collective-permute-start(bf16[1024,1024]{1,0:T(8,128)(2,1)} %get-tuple-element.250.refs_6_), channel_id=1, source_target_pairs={{0,4},{4,0},{8,12},{12,8},{16,20},{20,16},{24,28},{28,24},{1,5},{5... | collective-permute-start | bytes 6291464 | tf_op jit(solution)/shard_map/ppermute | solution.py:1154
  341.7 26.5 %collective-permute-start.42 = (bf16[512,384]{1,0:T(8,128)(2,1)}, bf16[512,384]{1,0:T(8,128)(2,1)S(1)}, u32[]{:S(2)}, u32[]{:S(2)}) collective-permute-start(bf16[512,384]{1,0:T(8,128)(2,1)} %get-tuple-element.243), channel_id=1, source_target_pairs={{0,16},{4,20},{8,24},{12,28},{16,0},{20,4},{24,8},{28,12},{1,17},{... | collective-permute-start | bytes 1179656 | tf_op jit(solution)/shard_map/ppermute | solution.py:1154
  344.7 23.6 %collective-permute-start.43 = (bf16[512,384]{1,0:T(8,128)(2,1)S(1)}, bf16[512,384]{1,0:T(8,128)(2,1)S(1)}, u32[]{:S(2)}, u32[]{:S(2)}) collective-permute-start(bf16[512,384]{1,0:T(8,128)(2,1)S(1)} %get-tuple-element.244), channel_id=1, source_target_pairs={{0,24},{4,28},{8,16},{12,20},{16,8},{20,12},{24,0},{28,4},{1,25},{... | collective-permute-start | bytes 1179656 | tf_op jit(solution)/shard_map/ppermute | solution.py:1154
  372.6 17.6 %collective-permute-start.44 = (bf16[256,2048]{1,0:T(8,128)(2,1)}, bf16[256,2048]{1,0:T(8,128)(2,1)}, u32[]{:S(2)}, u32[]{:S(2)}) collective-permute-start(bf16[256,2048]{1,0:T(8,128)(2,1)} %get-tuple-element.248.refs_2_), channel_id=1, source_target_pairs={{0,1},{1,0},{2,3},{3,2},{4,5},{5,4},{6,7},{7,6},{8,9},{9,8},{10,11... | collective-permute-start | bytes 3145736 | tf_op jit(solution)/shard_map/ppermute | solution.py:1157
  372.6 38.1 %collective-permute-start.49 = (bf16[3,128,2048]{2,1,0:T(8,128)(2,1)S(1)}, bf16[3,128,2048]{2,1,0:T(8,128)(2,1)}, u32[]{:S(2)}, u32[]{:S(2)}) collective-permute-start(bf16[3,128,2048]{2,1,0:T(8,128)(2,1)S(1)} %stack_rows.1.refs_6_.refs_3_), channel_id=1, source_target_pairs={{0,1},{1,0},{2,3},{3,2},{4,5},{5,4},{6,7},{7,6},{8,9},{9,8},{10,11... | collective-permute-start | bytes 4718600 | tf_op jit(solution)/shard_map/ppermute | solution.py:1157
  373.2 38.3 %collective-permute-start.50 = (bf16[3,128,2048]{2,1,0:T(8,128)(2,1)}, bf16[3,128,2048]{2,1,0:T(8,128)(2,1)}, u32[]{:S(2)}, u32[]{:S(2)}) collective-permute-start(bf16[3,128,2048]{2,1,0:T(8,128)(2,1)} %collective-permute-done.37.refs_5_), channel_id=1, source_target_pairs={{0,1},{1,0},{2,3},{3,2},{4,5},{5,4},{6,7},{7,6},{8,9},{9,8},{10,11... | collective-permute-start | bytes 4718600 | tf_op jit(solution)/shard_map/ppermute | solution.py:1157
  373.2 75.1 %collective-permute-start.55 = (bf16[512,1024]{1,0:T(8,128)(2,1)}, bf16[512,1024]{1,0:T(8,128)(2,1)}, u32[]{:S(2)}, u32[]{:S(2)}) collective-permute-start(bf16[512,1024]{1,0:T(8,128)(2,1)} %get-tuple-element.277), channel_id=1, source_target_pairs={{0,16},{4,20},{8,24},{12,28},{16,0},{20,4},{24,8},{28,12},{1,17},{... | collective-permute-start | bytes 3145736 | tf_op jit(solution)/shard_map/ppermute | solution.py:1154
  403.8 32.9 %collective-permute-start.47 = (bf16[1024,512]{1,0:T(8,128)(2,1)}, bf16[1024,512]{1,0:T(8,128)(2,1)}, u32[]{:S(2)}, u32[]{:S(2)}) collective-permute-start(bf16[1024,512]{1,0:T(8,128)(2,1)} %copy-done.37), channel_id=1, source_target_pairs={{0,4},{4,0},{8,12},{12,8},{16,20},{20,16},{24,28},{28,24},{1,5},{5... | collective-permute-start | bytes 3145736 | tf_op jit(solution)/shard_map/ppermute | solution.py:1154
  408.7 24.8 %collective-permute-start.48 = (bf16[256,1024]{1,0:T(8,128)(2,1)}, bf16[256,1024]{1,0:T(8,128)(2,1)}, u32[]{:S(2)}, u32[]{:S(2)}) collective-permute-start(bf16[256,1024]{1,0:T(8,128)(2,1)} %get-tuple-element.262), channel_id=1, source_target_pairs={{0,8},{4,12},{8,0},{12,4},{16,24},{20,28},{24,16},{28,20},{1,9},{5... | collective-permute-start | bytes 1572872 | tf_op jit(solution)/shard_map/ppermute | solution.py:1154
  410.7 29.9 %collective-permute-start.46 = (bf16[128,2048]{1,0:T(8,128)(2,1)}, bf16[128,2048]{1,0:T(8,128)(2,1)S(1)}, u32[]{:S(2)}, u32[]{:S(2)}) collective-permute-start(bf16[128,2048]{1,0:T(8,128)(2,1)} %get-tuple-element.259.refs_0_), channel_id=1, source_target_pairs={{0,2},{1,3},{2,0},{3,1},{4,6},{5,7},{6,4},{7,5},{8,10},{9,11},{10,... | collective-permute-start | bytes 1572872 | tf_op jit(solution)/shard_map/ppermute | solution.py:1157
  411.4 59.1 %collective-permute-start.53 = (bf16[512,1024]{1,0:T(8,128)(2,1)}, bf16[512,1024]{1,0:T(8,128)(2,1)}, u32[]{:S(2)}, u32[]{:S(2)}) collective-permute-start(bf16[512,1024]{1,0:T(8,128)(2,1)} %get-tuple-element.273), channel_id=1, source_target_pairs={{0,16},{4,20},{8,24},{12,28},{16,0},{20,4},{24,8},{28,12},{1,17},{... | collective-permute-start | bytes 3145736 | tf_op jit(solution)/shard_map/ppermute | solution.py:1154
  444.4 48.4 %collective-permute-start.52 = (bf16[256,2048]{1,0:T(8,128)(2,1)S(1)}, bf16[256,2048]{1,0:T(8,128)(2,1)S(1)}, u32[]{:S(2)}, u32[]{:S(2)}) collective-permute-start(bf16[256,2048]{1,0:T(8,128)(2,1)S(1)} %copy-done.98), channel_id=1, source_target_pairs={{0,8},{4,12},{8,0},{12,4},{16,24},{20,28},{24,16},{28,20},{1,9},{5... | collective-permute-start | bytes 3145736 | tf_op jit(solution)/shard_map/ppermute | solution.py:1154
  444.5 19.5 %collective-permute-start.54 = (bf16[1024,384]{1,0:T(8,128)(2,1)S(1)}, bf16[1024,384]{1,0:T(8,128)(2,1)S(1)}, u32[]{:S(2)}, u32[]{:S(2)}) collective-permute-start(bf16[1024,384]{1,0:T(8,128)(2,1)S(1)} %get-tuple-element.276.refs_3_), channel_id=1, source_target_pairs={{0,4},{4,0},{8,12},{12,8},{16,20},{20,16},{24,28},{28,24},{1,5},{5... | collective-permute-start | bytes 2359304 | tf_op jit(solution)/shard_map/ppermute | solution.py:1154
  493.1 30.4 %collective-permute-start.59 = (bf16[256,2048]{1,0:T(8,128)(2,1)S(1)}, bf16[256,2048]{1,0:T(8,128)(2,1)S(1)}, u32[]{:S(2)}, u32[]{:S(2)}) collective-permute-start(bf16[256,2048]{1,0:T(8,128)(2,1)S(1)} %row_sum.9.refs_3_.refs_0_), channel_id=1, source_target_pairs={{0,2},{1,3},{2,0},{3,1},{4,6},{5,7},{6,4},{7,5},{8,10},{9,11},{10,... | collective-permute-start | bytes 3145736 | tf_op jit(solution)/shard_map/ppermute | solution.py:1157
  495.3 23.7 %collective-permute-start.62 = (bf16[256,1024]{1,0:T(8,128)(2,1)S(1)}, bf16[256,1024]{1,0:T(8,128)(2,1)S(1)}, u32[]{:S(2)}, u32[]{:S(2)}) collective-permute-start(bf16[256,1024]{1,0:T(8,128)(2,1)S(1)} %get-tuple-element.295), channel_id=1, source_target_pairs={{0,8},{4,12},{8,0},{12,4},{16,24},{20,28},{24,16},{28,20},{1,9},{5... | collective-permute-start | bytes 1572872 | tf_op jit(solution)/shard_map/ppermute | solution.py:1154
  495.3 25.8 %collective-permute-start.60 = (bf16[512,512]{1,0:T(8,128)(2,1)S(1)}, bf16[512,512]{1,0:T(8,128)(2,1)S(1)}, u32[]{:S(2)}, u32[]{:S(2)}) collective-permute-start(bf16[512,512]{1,0:T(8,128)(2,1)S(1)} %get-tuple-element.293), channel_id=1, source_target_pairs={{0,16},{4,20},{8,24},{12,28},{16,0},{20,4},{24,8},{28,12},{1,17},{... | collective-permute-start | bytes 1572872 | tf_op jit(solution)/shard_map/ppermute | solution.py:1154
  523.9 27.7 %collective-permute-start.63 = (bf16[256,2048]{1,0:T(8,128)(2,1)S(1)}, bf16[256,2048]{1,0:T(8,128)(2,1)}, u32[]{:S(2)}, u32[]{:S(2)}) collective-permute-start(bf16[256,2048]{1,0:T(8,128)(2,1)S(1)} %add_rows.1.refs_3_.refs_1_), channel_id=1, source_target_pairs={{0,1},{1,0},{2,3},{3,2},{4,5},{5,4},{6,7},{7,6},{8,9},{9,8},{10,11... | collective-permute-start | bytes 3145736 | tf_op jit(solution)/shard_map/ppermute | solution.py:1157
  523.9 23.4 %collective-permute-start.64 = (bf16[256,1024]{1,0:T(8,128)(2,1)}, bf16[256,1024]{1,0:T(8,128)(2,1)S(1)}, u32[]{:S(2)}, u32[]{:S(2)}) collective-permute-start(bf16[256,1024]{1,0:T(8,128)(2,1)} %get-tuple-element.298), channel_id=1, source_target_pairs={{0,8},{4,12},{8,0},{12,4},{16,24},{20,28},{24,16},{28,20},{1,9},{5... | collective-permute-start | bytes 1572872 | tf_op jit(solution)/shard_map/ppermute | solution.py:1154
  524.0 31.8 %collective-permute-start.69 = (bf16[256,512]{1,0:T(8,128)(2,1)}, bf16[256,512]{1,0:T(8,128)(2,1)}, u32[]{:S(2)}, u32[]{:S(2)}) collective-permute-start(bf16[256,512]{1,0:T(8,128)(2,1)} %get-tuple-element.307), channel_id=1, source_target_pairs={{0,8},{4,12},{8,0},{12,4},{16,24},{20,28},{24,16},{28,20},{1,9},{5... | collective-permute-start | bytes 786440 | tf_op jit(solution)/shard_map/ppermute | solution.py:1154
  526.9 31.1 %collective-permute-start.65 = (bf16[256,384]{1,0:T(8,128)(2,1)}, bf16[256,384]{1,0:T(8,128)(2,1)}, u32[]{:S(2)}, u32[]{:S(2)}) collective-permute-start(bf16[256,384]{1,0:T(8,128)(2,1)} %copy-done.82), channel_id=1, source_target_pairs={{0,8},{4,12},{8,0},{12,4},{16,24},{20,28},{24,16},{28,20},{1,9},{5... | collective-permute-start | bytes 589832 | tf_op jit(solution)/shard_map/ppermute | solution.py:1154
  542.5 18.0 %collective-permute-start.66 = (bf16[256,384]{1,0:T(8,128)(2,1)}, bf16[256,384]{1,0:T(8,128)(2,1)}, u32[]{:S(2)}, u32[]{:S(2)}) collective-permute-start(bf16[256,384]{1,0:T(8,128)(2,1)} %copy-done.81), channel_id=1, source_target_pairs={{0,16},{4,20},{8,24},{12,28},{16,0},{20,4},{24,8},{28,12},{1,17},{... | collective-permute-start | bytes 589832 | tf_op jit(solution)/shard_map/ppermute | solution.py:1154
  (123 other events, 1485.0 us)
where the time goes:
time: 577 us; the launch traced here: 566 us
  Pallas kernels  223 us (39%)
  waiting for transfers between devices  180 us (31%)
  starting transfers between devices  91.5 us (16%)
  local copies, waits for them, and re-layouts  52.9 us (9%)
  other arithmetic  16.6 us (3%)
    pallas_call x52, Pallas kernels, call(): pl.pallas_call(kernel, out_shape=out_shape, compiler_params=pltpu.Compile...  223 us
    ppermute x45, waiting for transfers between devices, seq_swap(): return lax.ppermute(v, 'seq', [(i, i ^ distance) for i in range(n_seq)])  153 us
    ppermute x45, starting transfers between devices, seq_swap(): return lax.ppermute(v, 'seq', [(i, i ^ distance) for i in range(n_seq)])  77 us
    unnamed x201, local copies, waits for them, and re-layouts  33.6 us
    ppermute x26, waiting for transfers between devices, mp_swap(): return lax.ppermute(v, 'mp', [(i, i ^ distance) for i in range(n_mp)])  26.9 us
    ppermute x26, starting transfers between devices, mp_swap(): return lax.ppermute(v, 'mp', [(i, i ^ distance) for i in range(n_mp)])  14.4 us
  transfers between devices with their start and end apart: 71, of which 26 were waited for; matrix products, arithmetic and copies ran while one was open for 6% of the time, Pallas kernels for 35%

commit v1 on v0

--- a/solution.py
+++ b/solution.py
@@ -17,6 +17,7 @@
 CHUNKS = 2
 SHARE = 0.5
 ORDER = []
+LOOSE = [False]
 MIB = 1024 * 1024
 F32 = jnp.float32
 BF16 = jnp.bfloat16
@@ -49,6 +50,7 @@
     **kwargs,
 ):
     n = prefetch + len(in_specs)
+    chain = chain and not LOOSE[0]
     after = list(after) + (ORDER if chain else [])
 
     def kernel(*refs):
@@ -82,9 +84,17 @@
 
 def hold(values, after=()):
     n = len(values)
+    if LOOSE[0]:
+        return list(lax.optimization_barrier((*values, *after))[:n])
     made = lax.optimization_barrier((*values, *ORDER, *after))
     ORDER[:] = made[n : n + len(ORDER)]
     return list(made[:n])
+
+
+def loose(step, *args):
+    LOOSE[0] = True
+    step(*args)
+    LOOSE[0] = False
 
 
 def whole(memory):
@@ -1535,40 +1545,40 @@
 
     heads_out()
     dact_own()
+    gather_z(1)
     out_sum()
     swap_weights()
     norm_chunk(1)
     dact_sib()
     norm_chunk(0)
     turn_cot()
+    swap_cot()
+    gather_z(2)
     hidden_sib()
-    gather_z(2)
-    gather_z(1)
-    swap_cot()
     swap_dg()
+    hidden_own()
+    turn_normed()
     swap_du()
-    turn_normed()
     swap_normed()
-    hidden_own()
     grad_down()
     hidden_in()
     send_down()
+    grad_gate()
     gather_z(3)
-    grad_gate()
     back_chunk(1)
     send_gate()
     back_chunk(0)
+    gather_x()
     norm_back_chunk(1)
     norm_back_chunk(0)
-    gather_x()
     heads_in()
     merge_down()
+    turn_branch()
     high_down()
     grad_up()
-    turn_branch()
     attend_far()
+    send_up()
     gather_core()
-    send_up()
     attend_near()
     merge_gate()
     high_gate()
@@ -1576,37 +1586,37 @@
     head_grads()
     pair_down()
     rows_in()
+    merge_up()
     grad_out()
-    merge_up()
-    high_up()
+    loose(high_up)
     in_sum()
     down_rows()
+    norm_in_chunk(0)
     send_out()
-    norm_in_chunk(0)
     turn_rows()
+    lay_down()
     grad_qkv()
-    lay_down()
     merge_out()
     high_out()
     norm_in_chunk(1)
     pair_rows()
     send_qkv()
     sum_gate()
-    join_in()
     gains_core()
     gains_seq(0)
     pair_gate()
+    join_in()
     split_qkv()
     sum_up()
+    sum_rows()
+    gains_seq(2)
     pair_up()
-    sum_rows()
+    sum_out()
+    lay_gate()
+    loose(add_out)
     lay_up()
-    gains_seq(2)
-    sum_out()
-    add_out()
-    lay_gate()
+    gains_seq(1)
     join_out()
-    gains_seq(1)
     lay_qkv()
     for bit in range(3, bits):
         gains_seq(bit)

time: 577 us -> 572 us (level)
    ppermute x26, waiting for transfers between devices: 26.9 us -> 42.3 us  [mp_swap(): return lax.ppermute(v, 'mp', [(i, i ^ distance) for i in range(n_mp)])]
    ppermute x45, waiting for transfers between devices: 153 us -> 142 us  [seq_swap(): return lax.ppermute(v, 'seq', [(i, i ^ distance) for i in range(n_seq)])]
    unnamed x201 -> x197, local copies, waits for them, and re-layouts: 33.6 us -> 27.2 us
  transfers between devices with their start and end apart: 71 -> 71, of which waited for: 26 -> 27; matrix products, arithmetic and copies ran while one was open for 6% -> 6% of each run, Pallas kernels for 35% -> 38%
where the time goes in v1:
time: 572 us; the launch traced here: 562 us
  Pallas kernels  225 us (39%)
  waiting for transfers between devices  184 us (32%)
  starting transfers between devices  86.4 us (15%)
  local copies, waits for them, and re-layouts  51.1 us (9%)
  other arithmetic  13 us (2%)
    pallas_call x52, Pallas kernels, call(): pl.pallas_call(kernel, out_shape=out_shape, compiler_params=pltpu.Compile...  225 us
    ppermute x45, waiting for transfers between devices, seq_swap(): return lax.ppermute(v, 'seq', [(i, i ^ distance) for i in range(n_seq)])  142 us
    ppermute x45, starting transfers between devices, seq_swap(): return lax.ppermute(v, 'seq', [(i, i ^ distance) for i in range(n_seq)])  73 us
    ppermute x26, waiting for transfers between devices, mp_swap(): return lax.ppermute(v, 'mp', [(i, i ^ distance) for i in range(n_mp)])  42.3 us
    unnamed x197, local copies, waits for them, and re-layouts  27.2 us
    ppermute x26, starting transfers between devices, mp_swap(): return lax.ppermute(v, 'mp', [(i, i ^ distance) for i in range(n_mp)])  13.4 us
  transfers between devices with their start and end apart: 71, of which 27 were waited for; matrix products, arithmetic and copies ran while one was open for 6% of the time, Pallas kernels for 38%

profile of v1, /device:TPU:0, one launch (start us, length us, event | category | flops | bytes accessed | tf_op | source)
XLA Modules:
  0.0 562.1 jit_solution(6286847375077891970)
XLA Ops:
  5.3 8.7 %project_qkv.2 = (bf16[512,384]{1,0:T(8,128)(2,1)}, bf16[512,384]{1,0:T(8,128)(2,1)}, bf16[512,2048]{1,0:T(8,128)(2,1)}) custom-call(s32[4]{0:T(128)} %pad_add_fusion.refs_0_, bf16[512,2048]{1,0:T(8,128)(2,1)} %refs_1_.4, f32[1,2048]{1,0:T(1,128)} %bitcast.42, bf16[2048,512]{1,0:T(8,128)(2,1)} %refs_5_.13, bf16[2048,512]{1,0:T(8,128)(2,1)} %refs_6_.3, ...), custom_call_target="tpu_custom_call" | custom-call | flops 3221225472 | bytes 16252928 | tf_op jit(solution)/shard_map/project_qkv/pallas_call | solution.py:69
  14.0 4.0 collective-permute-start.1
  18.0 7.3 %project_qkv.3 = (bf16[512,384]{1,0:T(8,128)(2,1)}, bf16[512,384]{1,0:T(8,128)(2,1)}) custom-call(s32[4]{0:T(128)} %pad_add_fusion.refs_0_, bf16[512,2048]{1,0:T(8,128)(2,1)} %get-tuple-element.158.refs_1_.refs_2_, bf16[2048,512]{1,0:T(8,128)(2,1)} %refs_5_.13, bf16[2048,512]{1,0:T(8,128)(2,1)} %refs_6_.3, bf16[2048,512]{1,0:T(8,128)(2,1)} %refs_7_.3, ...), custom_call_target="tpu_custom_call" | custom-call | flops 3221225472 | bytes 16252928 | tf_op jit(solution)/shard_map/project_qkv/pallas_call | solution.py:69
  30.3 7.7 %constant_dynamic-slice_fusion.5 = (bf16[2048,1024]{1,0:T(8,128)(2,1)}, bf16[2048,1024]{1,0:T(8,128)(2,1)}) fusion(bf16[2048,2048]{1,0:T(8,128)(2,1)} %refs_7_.2, s32[]{:T(128)S(6)} %select_n.39, bf16[2048,2048]{1,0:T(8,128)(2,1)} %refs_5_.11), kind=kLoop, calls=%fused_computation.22 | loop fusion | bytes 16777220 | tf_op jit(solution)/shard_map/dynamic_slice | solution.py:1216
  38.0 13.7 %collective-permute-done.refs_3_.refs_7_.refs_11_ = bf16[512,384]{1,0:T(8,128)(2,1)S(1)} collective-permute-done((bf16[512,384]{1,0:T(8,128)(2,1)}, bf16[512,384]{1,0:T(8,128)(2,1)S(1)}, u32[]{:S(2)}, u32[]{:S(2)}) %collective-permute-start) | collective-permute-done | bytes 393248 | tf_op jit(solution)/shard_map/ppermute | solution.py:1164
  57.6 4.8 constant_dynamic-slice_fusion.7
  63.5 4.2 collective-permute-done.5.refs_12_
  67.7 3.9 collective-permute-done.6.refs_13_
  72.7 16.5 %attend.1 = (bf16[512,128]{1,0:T(8,128)(2,1)S(1)}, bf16[512,128]{1,0:T(8,128)(2,1)S(1)}, bf16[512,128]{1,0:T(8,128)(2,1)S(1)}, bf16[512,128]{1,0:T(8,128)(2,1)S(1)}) custom-call(s32[4]{0:T(128)S(1)} %copy-done.65, s32[5]{0:T(128)S(1)} %copy-done.66, bf16[512,384]{1,0:T(8,128)(2,1)S(1)} %copy-done.56, ...), custom_call_target="tpu_custom_call" | custom-call | flops 8589934592 | bytes 6291456 | tf_op jit(solution)/shard_map/attend/pallas_call | solution.py:69
  95.6 5.6 collective-permute-done.8.refs_3_
  106.7 6.2 %hidden_upstream.2.refs_2_.refs_7_ = bf16[512,1024]{1,0:T(8,128)(2,1)} custom-call(s32[4]{0:T(128)S(1)} %copy-done.65, bf16[128,2048]{1,0:T(8,128)(2,1)S(1)} %get-tuple-element.332.refs_1_.refs_2_.refs_3_, bf16[128,2048]{1,0:T(8,128)(2,1)S(1)} %get-tuple-element.331.refs_2_.refs_3_, bf16[128,2048]{1,0:T(8,128)(2,1)S(1)} %get-tuple-element.330.refs_3_.refs_4_, ...), custom_call_target="tpu_custom_call" | custom-call | flops 4294967296 | bytes 16777216 | tf_op jit(solution)/shard_map/hidden_upstream/pallas_call | solution.py:69
  118.9 11.7 %collective-permute-done.14.refs_1_ = bf16[128,2048]{1,0:T(8,128)(2,1)} collective-permute-done((bf16[128,2048]{1,0:T(8,128)(2,1)}, bf16[128,2048]{1,0:T(8,128)(2,1)}, u32[]{:S(2)}, u32[]{:S(2)}) %collective-permute-start.14) | collective-permute-done | bytes 524320 | tf_op jit(solution)/shard_map/ppermute | solution.py:1167
  135.3 5.7 %hidden_upstream.3.refs_4_.refs_7_ = bf16[512,1024]{1,0:T(8,128)(2,1)} custom-call(s32[4]{0:T(128)S(1)} %copy-done.65, bf16[128,2048]{1,0:T(8,128)(2,1)S(1)} %get-tuple-element.332.refs_1_.refs_2_.refs_3_, bf16[128,2048]{1,0:T(8,128)(2,1)S(1)} %get-tuple-element.331.refs_2_.refs_3_, bf16[128,2048]{1,0:T(8,128)(2,1)S(1)} %get-tuple-element.330.refs_3_.refs_4_, ...), custom_call_target="tpu_custom_call" | custom-call | flops 4294967296 | bytes 16777216 | tf_op jit(solution)/shard_map/hidden_upstream/pallas_call | solution.py:69
  147.6 10.3 %collective-permute-done.15.refs_3_.refs_4_ = bf16[128,2048]{1,0:T(8,128)(2,1)S(1)} collective-permute-done((bf16[128,2048]{1,0:T(8,128)(2,1)S(1)}, bf16[128,2048]{1,0:T(8,128)(2,1)S(1)}, u32[]{:S(2)}, u32[]{:S(2)}) %collective-permute-start.15) | collective-permute-done | bytes 524320 | tf_op jit(solution)/shard_map/ppermute | solution.py:1164
  157.9 10.0 %hidden.2 = (bf16[512,1024]{1,0:T(8,128)(2,1)}, bf16[512,1024]{1,0:T(8,128)(2,1)}, bf16[512,1024]{1,0:T(8,128)(2,1)}) custom-call(s32[4]{0:T(128)S(1)} %copy-done.65, bf16[128,2048]{1,0:T(8,128)(2,1)S(1)} %get-tuple-element.180.refs_1_.refs_2_, bf16[128,2048]{1,0:T(8,128)(2,1)S(1)} %get-tuple-element.181.refs_2_.refs_3_, ...), custom_call_target="tpu_custom_call" | custom-call | flops 8589934592 | bytes 29360128 | tf_op jit(solution)/shard_map/hidden/pallas_call | solution.py:69
  169.9 10.8 %hidden.3 = (bf16[512,1024]{1,0:T(8,128)(2,1)}, bf16[512,1024]{1,0:T(8,128)(2,1)}, bf16[512,1024]{1,0:T(8,128)(2,1)}) custom-call(s32[4]{0:T(128)S(1)} %copy-done.65, bf16[128,2048]{1,0:T(8,128)(2,1)S(1)} %get-tuple-element.180.refs_1_.refs_2_, bf16[128,2048]{1,0:T(8,128)(2,1)S(1)} %get-tuple-element.181.refs_2_.refs_3_, ...), custom_call_target="tpu_custom_call" | custom-call | flops 8589934592 | bytes 29360128 | tf_op jit(solution)/shard_map/hidden/pallas_call | solution.py:69
  185.1 8.6 %weight_grad.5 = (bf16[1024,1024]{1,0:T(8,128)(2,1)}, bf16[1024,1024]{1,0:T(8,128)(2,1)}) custom-call(bf16[2048,512]{1,0:T(8,128)(2,1)} %copy-done.31, bf16[2048,512]{1,0:T(8,128)(2,1)} %collective-permute-done.19.refs_1_, bf16[512,1024]{1,0:T(8,128)(2,1)S(1)} %copy-done.45, bf16[512,1024]{1,0:T(8,128)(2,1)} %collective-permute-done.20.refs_3_, ...), custom_call_target="tpu_custom_call" | custom-call | flops 8589934592 | bytes 20971520 | tf_op jit(solution)/shard_map/weight_grad/pallas_call | solution.py:69
  193.7 15.6 %hidden_back.1 = (bf16[128,2048]{1,0:T(8,128)(2,1)S(1)}, bf16[128,2048]{1,0:T(8,128)(2,1)S(1)}, bf16[128,2048]{1,0:T(8,128)(2,1)S(1)}, bf16[128,2048]{1,0:T(8,128)(2,1)}) custom-call(s32[4]{0:T(128)S(1)} %copy-done.65, bf16[512,1024]{1,0:T(8,128)(2,1)} %get-tuple-element.191.refs_1_.refs_2_, bf16[512,1024]{1,0:T(8,128)(2,1)} %get-tuple-element.201.refs_2_, ...), custom_call_target="tpu_custom_call" | custom-call | flops 17179869184 | bytes 46137344 | tf_op jit(solution)/shard_map/hidden_back/pallas_call | solution.py:69
  211.3 4.9 collective-permute-start.36
  216.2 8.7 %weight_grad.6 = (bf16[1024,1024]{1,0:T(8,128)(2,1)}, bf16[1024,1024]{1,0:T(8,128)(2,1)}) custom-call(bf16[2048,512]{1,0:T(8,128)(2,1)} %copy-done.26, bf16[2048,512]{1,0:T(8,128)(2,1)} %copy-done.94, bf16[512,1024]{1,0:T(8,128)(2,1)S(1)} %copy-done.84, bf16[512,1024]{1,0:T(8,128)(2,1)} %collective-permute-done.23.refs_3_, ...), custom_call_target="tpu_custom_call" | custom-call | flops 8589934592 | bytes 20971520 | tf_op jit(solution)/shard_map/weight_grad/pallas_call | solution.py:69
  230.7 4.8 collective-permute-done.21.refs_1_
  237.3 8.7 %collective-permute-done.29.refs_2_ = bf16[128,2048]{1,0:T(8,128)(2,1)} collective-permute-done((bf16[128,2048]{1,0:T(8,128)(2,1)}, bf16[128,2048]{1,0:T(8,128)(2,1)}, u32[]{:S(2)}, u32[]{:S(2)}) %collective-permute-start.29) | collective-permute-done | bytes 524320 | tf_op jit(solution)/shard_map/ppermute | solution.py:1164
  250.2 3.2 collective-permute-done.26.refs_1_
  256.0 5.9 %fusion = (f32[4,512,64]{2,1,0:T(8,128)}, f32[4,512,64]{2,1,0:T(8,128)}, f32[4,512,64]{2,1,0:T(8,128)}) fusion(f32[64]{0:T(128)S(1)} %copy-done.93, f32[4,512]{1,0:T(4,128)S(1)} %subtract_convert_fusion), kind=kLoop, calls=%fused_computation.9 | loop fusion | flops 262144 | bytes 1581312 | tf_op jit(solution)/shard_map/neg | solution.py:1120
  271.6 3.7 merge.4
  283.0 8.6 %weight_grad.7 = (bf16[1024,1024]{1,0:T(8,128)(2,1)}, bf16[1024,1024]{1,0:T(8,128)(2,1)}) custom-call(bf16[2048,512]{1,0:T(8,128)(2,1)} %copy-done.26, bf16[2048,512]{1,0:T(8,128)(2,1)} %copy-done.94, bf16[512,1024]{1,0:T(8,128)(2,1)S(1)} %copy-done.83, bf16[512,1024]{1,0:T(8,128)(2,1)} %collective-permute-done.35.refs_3_, bf16[2048,512]{1,0:T(8,128)(2,1)} %copy-done.28), custom_call_target="tpu_custom_call" | custom-call | flops 8589934592 | bytes 20971520 | tf_op jit(solution)/shard_map/weight_grad/pallas_call | solution.py:69
  291.7 9.0 %attend_back.2 = (f32[4,512,128]{2,1,0:T(8,128)S(1)}, bf16[4,512,256]{2,1,0:T(8,128)(2,1)S(1)}) custom-call(s32[4]{0:T(128)S(1)} %copy-done.65, s32[5]{0:T(128)S(1)} %copy-done.67, bf16[512,384]{1,0:T(8,128)(2,1)S(1)} %copy-done.57, bf16[512,384]{1,0:T(8,128)(2,1)S(1)} %copy-done.59, bf16[512,384]{1,0:T(8,128)(2,1)S(1)} %collective-permute-done.1.refs_4_.refs_8_.refs_12_, ...), custom_call_target="tpu_custom_call" | custom-call | flops 10737418240 | bytes 6291456 | tf_op jit(solution)/shard_map/attend_back/pallas_call | solution.py:69
  300.6 7.6 %collective-permute-start.38 = (bf16[4,512,256]{2,1,0:T(8,128)(2,1)S(1)}, bf16[4,512,256]{2,1,0:T(8,128)(2,1)S(1)}, u32[]{:S(2)}, u32[]{:S(2)}) collective-permute-start(bf16[4,512,256]{2,1,0:T(8,128)(2,1)S(1)} %get-tuple-element.231), channel_id=1, source_target_pairs={{0,4},{4,0},{8,12},{12,8},{16,20},{20,16},{24,28},{28,24},{1,5},{5... | collective-permute-start | bytes 3145736 | tf_op jit(solution)/shard_map/ppermute | solution.py:1164
  309.0 4.8 collective-permute-done.37.refs_5_
  313.8 13.2 %attend_back.3 = (f32[4,512,128]{2,1,0:T(8,128)S(1)}, f32[4,512,256]{2,1,0:T(8,128)S(1)}) custom-call(s32[4]{0:T(128)S(1)} %copy-done.65, s32[5]{0:T(128)S(1)} %copy-done.67, bf16[512,384]{1,0:T(8,128)(2,1)S(1)} %copy-done.57, bf16[512,384]{1,0:T(8,128)(2,1)S(1)} %copy-done.59, bf16[512,384]{1,0:T(8,128)(2,1)S(1)} %collective-permute-done.1.refs_4_.refs_8_.refs_12_, ...), custom_call_target="tpu_custom_call" | custom-call | flops 10737418240 | bytes 6291456 | tf_op jit(solution)/shard_map/attend_back/pallas_call | solution.py:69
  327.0 3.8 merge.5
  332.8 7.7 %collective-permute-done.38.refs_2_ = bf16[4,512,256]{2,1,0:T(8,128)(2,1)S(1)} collective-permute-done((bf16[4,512,256]{2,1,0:T(8,128)(2,1)S(1)}, bf16[4,512,256]{2,1,0:T(8,128)(2,1)S(1)}, u32[]{:S(2)}, u32[]{:S(2)}) %collective-permute-start.38) | collective-permute-done | bytes 1048608 | tf_op jit(solution)/shard_map/ppermute | solution.py:1164
  345.8 10.7 %collective-permute-done.41.refs_2_ = bf16[512,384]{1,0:T(8,128)(2,1)S(1)} collective-permute-done((bf16[512,384]{1,0:T(8,128)(2,1)S(1)}, bf16[512,384]{1,0:T(8,128)(2,1)S(1)}, u32[]{:S(2)}, u32[]{:S(2)}) %collective-permute-start.41) | collective-permute-done | bytes 393248 | tf_op jit(solution)/shard_map/ppermute | solution.py:1164
  356.5 15.2 %collective-permute-done.42.refs_3_ = bf16[512,384]{1,0:T(8,128)(2,1)S(1)} collective-permute-done((bf16[512,384]{1,0:T(8,128)(2,1)S(1)}, bf16[512,384]{1,0:T(8,128)(2,1)S(1)}, u32[]{:S(2)}, u32[]{:S(2)}) %collective-permute-start.42) | collective-permute-done | bytes 393248 | tf_op jit(solution)/shard_map/ppermute | solution.py:1164
  371.8 4.4 heads_project.3
  376.9 5.9 %collective-permute-start.57 = (bf16[512,1024]{1,0:T(8,128)(2,1)}, bf16[512,1024]{1,0:T(8,128)(2,1)}, u32[]{:S(2)}, u32[]{:S(2)}) collective-permute-start(bf16[512,1024]{1,0:T(8,128)(2,1)} %get-tuple-element.273), channel_id=1, source_target_pairs={{0,16},{4,20},{8,24},{12,28},{16,0},{20,4},{24,8},{28,12},{1,17},{... | collective-permute-start | bytes 3145736 | tf_op jit(solution)/shard_map/ppermute | solution.py:1164
  387.8 5.1 weight_grad.8
  396.0 9.2 %down.1 = (bf16[256,2048]{1,0:T(8,128)(2,1)S(1)}, bf16[256,2048]{1,0:T(8,128)(2,1)}) custom-call(s32[4]{0:T(128)S(1)} %copy-done.65, bf16[512,1024]{1,0:T(8,128)(2,1)} %get-tuple-element.190.refs_6_.refs_2_.refs_1_, bf16[512,1024]{1,0:T(8,128)(2,1)} %get-tuple-element.189.refs_8_.refs_2_, bf16[2048,2048]{1,0:T(8,128)(2,1)} %refs_3_.5, ...), custom_call_target="tpu_custom_call" | custom-call | flops 8589934592 | bytes 25165824 | tf_op jit(solution)/shard_map/down/pallas_call | solution.py:69
  414.3 10.0 %turn_all.1.refs_3_.refs_0_ = bf16[2048,2048]{1,0:T(8,128)(2,1)} custom-call(s32[1]{0:T(128)} %bitcast.2.refs_0_, s32[8]{0:T(128)S(1)} %broadcast_xor_fusion.refs_1_, bf16[512,2048]{1,0:T(8,128)(2,1)} %get-tuple-element.158.refs_1_.refs_2_, bf16[3,128,2048]{2,1,0:T(8,128)(2,1)} %copy-done.3, bf16[3,128,2048]{2,1,0:T(8,128)(2,1)} %collective-permute-done.49.refs_4_, ...), custom_call_target="tpu_custom_call" | custom-call | flops 4294967296 | bytes 33554432 | tf_op jit(solution)/shard_map/turn_all/pallas_call | solution.py:69
  424.3 3.4 copy-done.2
  427.7 3.3 lay.3.refs_2_
  431.0 7.7 %weight_grad.9 = (bf16[1024,384]{1,0:T(8,128)(2,1)S(1)}, bf16[1024,384]{1,0:T(8,128)(2,1)S(1)}) custom-call(bf16[2048,2048]{1,0:T(8,128)(2,1)} %turn_all.1.refs_3_.refs_0_, bf16[2048,384]{1,0:T(8,128)(2,1)} %pad_maximum_fusion.1.refs_1_, f32[2048,256]{1,0:T(8,128)} %lay.3.refs_2_), custom_call_target="tpu_custom_call" | custom-call | flops 6442450944 | bytes 23068672 | tf_op jit(solution)/shard_map/weight_grad/pallas_call | solution.py:69
  443.5 8.7 %collective-permute-done.57 = bf16[512,1024]{1,0:T(8,128)(2,1)} collective-permute-done((bf16[512,1024]{1,0:T(8,128)(2,1)}, bf16[512,1024]{1,0:T(8,128)(2,1)}, u32[]{:S(2)}, u32[]{:S(2)}) %collective-permute-start.57) | collective-permute-done | bytes 1048608 | tf_op jit(solution)/shard_map/ppermute | solution.py:1164
  461.8 12.5 %collective-permute-done.53 = bf16[512,1024]{1,0:T(8,128)(2,1)S(1)} collective-permute-done((bf16[512,1024]{1,0:T(8,128)(2,1)}, bf16[512,1024]{1,0:T(8,128)(2,1)S(1)}, u32[]{:S(2)}, u32[]{:S(2)}) %collective-permute-start.53) | collective-permute-done | bytes 1048608 | tf_op jit(solution)/shard_map/ppermute | solution.py:1164
  475.4 20.8 %collective-permute-done.52.refs_1_ = bf16[256,2048]{1,0:T(8,128)(2,1)S(1)} collective-permute-done((bf16[256,2048]{1,0:T(8,128)(2,1)S(1)}, bf16[256,2048]{1,0:T(8,128)(2,1)S(1)}, u32[]{:S(2)}, u32[]{:S(2)}) %collective-permute-start.52) | collective-permute-done | bytes 1048608 | tf_op jit(solution)/shard_map/ppermute | solution.py:1164
  502.9 18.2 %collective-permute-done.59.refs_1_ = bf16[256,2048]{1,0:T(8,128)(2,1)S(1)} collective-permute-done((bf16[256,2048]{1,0:T(8,128)(2,1)S(1)}, bf16[256,2048]{1,0:T(8,128)(2,1)S(1)}, u32[]{:S(2)}, u32[]{:S(2)}) %collective-permute-start.59) | collective-permute-done | bytes 1048608 | tf_op jit(solution)/shard_map/ppermute | solution.py:1167
  529.3 8.6 %collective-permute-done.62 = f32[2,2048]{1,0:T(2,128)S(1)} collective-permute-done((f32[2,2048]{1,0:T(2,128)}, f32[2,2048]{1,0:T(2,128)S(1)}, u32[]{:S(2)}, u32[]{:S(2)}) %collective-permute-start.62) | collective-permute-done | bytes 16416 | tf_op jit(solution)/shard_map/ppermute | solution.py:1164
  537.9 3.4 collective-permute-start.67
  (381 shorter events, 162.7 us)
Async XLA Ops:
  14.0 40.1 %collective-permute-start.1 = (bf16[512,384]{1,0:T(8,128)(2,1)}, bf16[512,384]{1,0:T(8,128)(2,1)S(1)}, u32[]{:S(2)}, u32[]{:S(2)}) collective-permute-start(bf16[512,384]{1,0:T(8,128)(2,1)} %get-tuple-element.159.refs_7_), channel_id=1, source_target_pairs={{0,16},{4,20},{8,24},{12,28},{16,0},{20,4},{24,8},{28,12},{1,17},{... | collective-permute-start | bytes 1179656 | tf_op jit(solution)/shard_map/ppermute | solution.py:1164
  25.3 26.4 %collective-permute-start = (bf16[512,384]{1,0:T(8,128)(2,1)}, bf16[512,384]{1,0:T(8,128)(2,1)S(1)}, u32[]{:S(2)}, u32[]{:S(2)}) collective-permute-start(bf16[512,384]{1,0:T(8,128)(2,1)} %get-tuple-element.161), channel_id=1, source_target_pairs={{0,8},{4,12},{8,0},{12,4},{16,24},{20,28},{24,16},{28,20},{1,9},{5... | collective-permute-start | bytes 1179656 | tf_op jit(solution)/shard_map/ppermute | solution.py:1164
  26.9 28.4 %collective-permute-start.2 = (bf16[512,384]{1,0:T(8,128)(2,1)}, bf16[512,384]{1,0:T(8,128)(2,1)S(1)}, u32[]{:S(2)}, u32[]{:S(2)}) collective-permute-start(bf16[512,384]{1,0:T(8,128)(2,1)} %get-tuple-element.162), channel_id=1, source_target_pairs={{0,24},{4,28},{8,16},{12,20},{16,8},{20,12},{24,0},{28,4},{1,25},{... | collective-permute-start | bytes 1179656 | tf_op jit(solution)/shard_map/ppermute | solution.py:1164
  28.6 34.9 %collective-permute-start.3 = (bf16[512,256]{1,0:T(8,128)(2,1)}, bf16[512,256]{1,0:T(8,128)(2,1)S(1)}, u32[]{:S(2)}, u32[]{:S(2)}) collective-permute-start(bf16[512,256]{1,0:T(8,128)(2,1)} %slice.44), channel_id=1, source_target_pairs={{0,4},{4,0},{8,12},{12,8},{16,20},{20,16},{24,28},{28,24},{1,5},{5... | collective-permute-start | bytes 786440 | tf_op jit(solution)/shard_map/ppermute | solution.py:1164
  56.0 15.6 %collective-permute-start.6 = (bf16[512,256]{1,0:T(8,128)(2,1)}, bf16[512,256]{1,0:T(8,128)(2,1)}, u32[]{:S(2)}, u32[]{:S(2)}) collective-permute-start(bf16[512,256]{1,0:T(8,128)(2,1)} %slice.60), channel_id=1, source_target_pairs={{0,4},{4,0},{8,12},{12,8},{16,20},{20,16},{24,28},{28,24},{1,5},{5... | collective-permute-start | bytes 786440 | tf_op jit(solution)/shard_map/ppermute | solution.py:1164
  63.5 37.6 %collective-permute-start.10 = (bf16[256,2048]{1,0:T(8,128)(2,1)}, bf16[256,2048]{1,0:T(8,128)(2,1)S(1)}, u32[]{:S(2)}, u32[]{:S(2)}) collective-permute-start(bf16[256,2048]{1,0:T(8,128)(2,1)} %constant_dynamic-slice_fusion.8), channel_id=1, source_target_pairs={{0,8},{4,12},{8,0},{12,4},{16,24},{20,28},{24,16},{28,20},{1,9},{5... | collective-permute-start | bytes 3145736 | tf_op jit(solution)/shard_map/ppermute | solution.py:1164
  115.1 20.2 %collective-permute-start.13 = (bf16[1024,2048]{1,0:T(8,128)(2,1)}, bf16[1024,2048]{1,0:T(8,128)(2,1)}, u32[]{:S(2)}, u32[]{:S(2)}) collective-permute-start(bf16[1024,2048]{1,0:T(8,128)(2,1)} %constant_dynamic-slice_fusion.7), channel_id=1, source_target_pairs={{0,1},{1,0},{2,3},{3,2},{4,5},{5,4},{6,7},{7,6},{8,9},{9,8},{10,11... | collective-permute-start | bytes 12582920 | tf_op jit(solution)/shard_map/ppermute | solution.py:1167
  115.1 32.5 %collective-permute-start.17 = (bf16[2048,1024]{1,0:T(8,128)(2,1)}, bf16[2048,1024]{1,0:T(8,128)(2,1)}, u32[]{:S(2)}, u32[]{:S(2)}) collective-permute-start(bf16[2048,1024]{1,0:T(8,128)(2,1)} %get-tuple-element.182), channel_id=1, source_target_pairs={{0,1},{1,0},{2,3},{3,2},{4,5},{5,4},{6,7},{7,6},{8,9},{9,8},{10,11... | collective-permute-start | bytes 12582920 | tf_op jit(solution)/shard_map/ppermute | solution.py:1167
  115.6 32.0 %collective-permute-start.18 = (bf16[2048,1024]{1,0:T(8,128)(2,1)}, bf16[2048,1024]{1,0:T(8,128)(2,1)}, u32[]{:S(2)}, u32[]{:S(2)}) collective-permute-start(bf16[2048,1024]{1,0:T(8,128)(2,1)} %get-tuple-element.183), channel_id=1, source_target_pairs={{0,1},{1,0},{2,3},{3,2},{4,5},{5,4},{6,7},{7,6},{8,9},{9,8},{10,11... | collective-permute-start | bytes 12582920 | tf_op jit(solution)/shard_map/ppermute | solution.py:1167
  117.2 24.2 %collective-permute-start.12 = (bf16[128,2048]{1,0:T(8,128)(2,1)S(1)}, bf16[128,2048]{1,0:T(8,128)(2,1)S(1)}, u32[]{:S(2)}, u32[]{:S(2)}) collective-permute-start(bf16[128,2048]{1,0:T(8,128)(2,1)S(1)} %get-tuple-element.178.refs_4_.refs_0_), channel_id=1, source_target_pairs={{0,2},{1,3},{2,0},{3,1},{4,6},{5,7},{6,4},{7,5},{8,10},{9,11},{10,... | collective-permute-start | bytes 1572872 | tf_op jit(solution)/shard_map/ppermute | solution.py:1167
  147.0 37.4 %collective-permute-start.19 = (bf16[2048,512]{1,0:T(8,128)(2,1)S(1)}, bf16[2048,512]{1,0:T(8,128)(2,1)}, u32[]{:S(2)}, u32[]{:S(2)}) collective-permute-start(bf16[2048,512]{1,0:T(8,128)(2,1)S(1)} %turn.3.refs_8_.refs_0_), channel_id=1, source_target_pairs={{0,1},{1,0},{2,3},{3,2},{4,5},{5,4},{6,7},{7,6},{8,9},{9,8},{10,11... | collective-permute-start | bytes 6291464 | tf_op jit(solution)/shard_map/ppermute | solution.py:1167
  168.0 15.9 %collective-permute-start.20 = (bf16[512,1024]{1,0:T(8,128)(2,1)}, bf16[512,1024]{1,0:T(8,128)(2,1)}, u32[]{:S(2)}, u32[]{:S(2)}) collective-permute-start(bf16[512,1024]{1,0:T(8,128)(2,1)} %get-tuple-element.189.refs_8_.refs_2_), channel_id=1, source_target_pairs={{0,1},{1,0},{2,3},{3,2},{4,5},{5,4},{6,7},{7,6},{8,9},{9,8},{10,11... | collective-permute-start | bytes 3145736 | tf_op jit(solution)/shard_map/ppermute | solution.py:1167
  168.0 69.3 %collective-permute-start.28 = (bf16[128,2048]{1,0:T(8,128)(2,1)}, bf16[128,2048]{1,0:T(8,128)(2,1)}, u32[]{:S(2)}, u32[]{:S(2)}) collective-permute-start(bf16[128,2048]{1,0:T(8,128)(2,1)} %constant_dynamic-slice_fusion.4), channel_id=1, source_target_pairs={{0,8},{4,12},{8,0},{12,4},{16,24},{20,28},{24,16},{28,20},{1,9},{5... | collective-permute-start | bytes 1572872 | tf_op jit(solution)/shard_map/ppermute | solution.py:1164
  169.7 55.2 %collective-permute-start.25 = (bf16[128,2048]{1,0:T(8,128)(2,1)}, bf16[128,2048]{1,0:T(8,128)(2,1)}, u32[]{:S(2)}, u32[]{:S(2)}) collective-permute-start(bf16[128,2048]{1,0:T(8,128)(2,1)} %constant_dynamic-slice_fusion.4), channel_id=1, source_target_pairs={{0,16},{4,20},{8,24},{12,28},{16,0},{20,4},{24,8},{28,12},{1,17},{... | collective-permute-start | bytes 1572872 | tf_op jit(solution)/shard_map/ppermute | solution.py:1164
  183.8 27.5 %collective-permute-start.22 = (bf16[2048,512]{1,0:T(8,128)(2,1)S(1)}, bf16[2048,512]{1,0:T(8,128)(2,1)S(1)}, u32[]{:S(2)}, u32[]{:S(2)}) collective-permute-start(bf16[2048,512]{1,0:T(8,128)(2,1)S(1)} %turn.4.refs_4_.refs_0_), channel_id=1, source_target_pairs={{0,1},{1,0},{2,3},{3,2},{4,5},{5,4},{6,7},{7,6},{8,9},{9,8},{10,11... | collective-permute-start | bytes 6291464 | tf_op jit(solution)/shard_map/ppermute | solution.py:1167
  183.9 27.1 %collective-permute-start.23 = (bf16[512,1024]{1,0:T(8,128)(2,1)S(1)}, bf16[512,1024]{1,0:T(8,128)(2,1)}, u32[]{:S(2)}, u32[]{:S(2)}) collective-permute-start(bf16[512,1024]{1,0:T(8,128)(2,1)S(1)} %copy-done.96), channel_id=1, source_target_pairs={{0,1},{1,0},{2,3},{3,2},{4,5},{5,4},{6,7},{7,6},{8,9},{9,8},{10,11... | collective-permute-start | bytes 3145736 | tf_op jit(solution)/shard_map/ppermute | solution.py:1167
  209.3 17.4 %collective-permute-start.24 = (bf16[128,2048]{1,0:T(8,128)(2,1)}, bf16[128,2048]{1,0:T(8,128)(2,1)S(1)}, u32[]{:S(2)}, u32[]{:S(2)}) collective-permute-start(bf16[128,2048]{1,0:T(8,128)(2,1)} %get-tuple-element.205), channel_id=1, source_target_pairs={{0,8},{4,12},{8,0},{12,4},{16,24},{20,28},{24,16},{28,20},{1,9},{5... | collective-permute-start | bytes 1572872 | tf_op jit(solution)/shard_map/ppermute | solution.py:1164
  211.1 24.5 %collective-permute-start.21 = (bf16[128,2048]{1,0:T(8,128)(2,1)S(1)}, bf16[128,2048]{1,0:T(8,128)(2,1)S(1)}, u32[]{:S(2)}, u32[]{:S(2)}) collective-permute-start(bf16[128,2048]{1,0:T(8,128)(2,1)S(1)} %get-tuple-element.199), channel_id=1, source_target_pairs={{0,8},{4,12},{8,0},{12,4},{16,24},{20,28},{24,16},{28,20},{1,9},{5... | collective-permute-start | bytes 1572872 | tf_op jit(solution)/shard_map/ppermute | solution.py:1164
  211.3 58.1 %collective-permute-start.36 = (bf16[1024,1024]{1,0:T(8,128)(2,1)}, bf16[1024,1024]{1,0:T(8,128)(2,1)}, u32[]{:S(2)}, u32[]{:S(2)}) collective-permute-start(bf16[1024,1024]{1,0:T(8,128)(2,1)} %get-tuple-element.221.refs_9_), channel_id=1, source_target_pairs={{0,4},{4,0},{8,12},{12,8},{16,20},{20,16},{24,28},{28,24},{1,5},{5... | collective-permute-start | bytes 6291464 | tf_op jit(solution)/shard_map/ppermute | solution.py:1164
  224.9 21.0 %collective-permute-start.29 = (bf16[128,2048]{1,0:T(8,128)(2,1)}, bf16[128,2048]{1,0:T(8,128)(2,1)}, u32[]{:S(2)}, u32[]{:S(2)}) collective-permute-start(bf16[128,2048]{1,0:T(8,128)(2,1)} %collective-permute-done.25.refs_1_), channel_id=1, source_target_pairs={{0,8},{4,12},{8,0},{12,4},{16,24},{20,28},{24,16},{28,20},{1,9},{5... | collective-permute-start | bytes 1572872 | tf_op jit(solution)/shard_map/ppermute | solution.py:1164
  229.2 18.2 %collective-permute-start.27 = (bf16[128,2048]{1,0:T(8,128)(2,1)}, bf16[128,2048]{1,0:T(8,128)(2,1)}, u32[]{:S(2)}, u32[]{:S(2)}) collective-permute-start(bf16[128,2048]{1,0:T(8,128)(2,1)} %row_sum.6.refs_2_.refs_0_), channel_id=1, source_target_pairs={{0,2},{1,3},{2,0},{3,1},{4,6},{5,7},{6,4},{7,5},{8,10},{9,11},{10,... | collective-permute-start | bytes 1572872 | tf_op jit(solution)/shard_map/ppermute | solution.py:1167
  235.7 17.7 %collective-permute-start.26 = (bf16[128,2048]{1,0:T(8,128)(2,1)S(1)}, bf16[128,2048]{1,0:T(8,128)(2,1)}, u32[]{:S(2)}, u32[]{:S(2)}) collective-permute-start(bf16[128,2048]{1,0:T(8,128)(2,1)S(1)} %row_sum.7.refs_3_.refs_0_), channel_id=1, source_target_pairs={{0,2},{1,3},{2,0},{3,1},{4,6},{5,7},{6,4},{7,5},{8,10},{9,11},{10,... | collective-permute-start | bytes 1572872 | tf_op jit(solution)/shard_map/ppermute | solution.py:1167
  237.2 45.7 %collective-permute-start.35 = (bf16[512,1024]{1,0:T(8,128)(2,1)}, bf16[512,1024]{1,0:T(8,128)(2,1)}, u32[]{:S(2)}, u32[]{:S(2)}) collective-permute-start(bf16[512,1024]{1,0:T(8,128)(2,1)} %get-tuple-element.219.refs_4_), channel_id=1, source_target_pairs={{0,1},{1,0},{2,3},{3,2},{4,5},{5,4},{6,7},{7,6},{8,9},{9,8},{10,11... | collective-permute-start | bytes 3145736 | tf_op jit(solution)/shard_map/ppermute | solution.py:1167
  269.4 57.6 %collective-permute-start.40 = (bf16[1024,1024]{1,0:T(8,128)(2,1)S(1)}, bf16[1024,1024]{1,0:T(8,128)(2,1)}, u32[]{:S(2)}, u32[]{:S(2)}) collective-permute-start(bf16[1024,1024]{1,0:T(8,128)(2,1)S(1)} %copy-done.20), channel_id=1, source_target_pairs={{0,4},{4,0},{8,12},{12,8},{16,20},{20,16},{24,28},{28,24},{1,5},{5... | collective-permute-start | bytes 6291464 | tf_op jit(solution)/shard_map/ppermute | solution.py:1164
  278.5 35.4 %collective-permute-start.37 = (bf16[3,128,2048]{2,1,0:T(8,128)(2,1)S(1)}, bf16[3,128,2048]{2,1,0:T(8,128)(2,1)}, u32[]{:S(2)}, u32[]{:S(2)}) collective-permute-start(bf16[3,128,2048]{2,1,0:T(8,128)(2,1)S(1)} %stack_rows.1.refs_5_.refs_3_), channel_id=1, source_target_pairs={{0,2},{1,3},{2,0},{3,1},{4,6},{5,7},{6,4},{7,5},{8,10},{9,11},{10,... | collective-permute-start | bytes 4718600 | tf_op jit(solution)/shard_map/ppermute | solution.py:1167
  281.3 49.4 %collective-permute-start.39 = (bf16[512,1024]{1,0:T(8,128)(2,1)}, bf16[512,1024]{1,0:T(8,128)(2,1)}, u32[]{:S(2)}, u32[]{:S(2)}) collective-permute-start(bf16[512,1024]{1,0:T(8,128)(2,1)} %get-tuple-element.232), channel_id=1, source_target_pairs={{0,16},{4,20},{8,24},{12,28},{16,0},{20,4},{24,8},{28,12},{1,17},{... | collective-permute-start | bytes 3145736 | tf_op jit(solution)/shard_map/ppermute | solution.py:1164
  300.6 39.9 %collective-permute-start.38 = (bf16[4,512,256]{2,1,0:T(8,128)(2,1)S(1)}, bf16[4,512,256]{2,1,0:T(8,128)(2,1)S(1)}, u32[]{:S(2)}, u32[]{:S(2)}) collective-permute-start(bf16[4,512,256]{2,1,0:T(8,128)(2,1)S(1)} %get-tuple-element.231), channel_id=1, source_target_pairs={{0,4},{4,0},{8,12},{12,8},{16,20},{20,16},{24,28},{28,24},{1,5},{5... | collective-permute-start | bytes 3145736 | tf_op jit(solution)/shard_map/ppermute | solution.py:1164
  308.9 75.1 %collective-permute-start.45 = (bf16[1024,1024]{1,0:T(8,128)(2,1)}, bf16[1024,1024]{1,0:T(8,128)(2,1)S(1)}, u32[]{:S(2)}, u32[]{:S(2)}) collective-permute-start(bf16[1024,1024]{1,0:T(8,128)(2,1)} %get-tuple-element.249.refs_14_), channel_id=1, source_target_pairs={{0,4},{4,0},{8,12},{12,8},{16,20},{20,16},{24,28},{28,24},{1,5},{5... | collective-permute-start | bytes 6291464 | tf_op jit(solution)/shard_map/ppermute | solution.py:1164
  341.9 29.8 %collective-permute-start.42 = (bf16[512,384]{1,0:T(8,128)(2,1)S(1)}, bf16[512,384]{1,0:T(8,128)(2,1)S(1)}, u32[]{:S(2)}, u32[]{:S(2)}) collective-permute-start(bf16[512,384]{1,0:T(8,128)(2,1)S(1)} %get-tuple-element.241), channel_id=1, source_target_pairs={{0,16},{4,20},{8,24},{12,28},{16,0},{20,4},{24,8},{28,12},{1,17},{... | collective-permute-start | bytes 1179656 | tf_op jit(solution)/shard_map/ppermute | solution.py:1164
  344.3 27.4 %collective-permute-start.43 = (bf16[512,384]{1,0:T(8,128)(2,1)S(1)}, bf16[512,384]{1,0:T(8,128)(2,1)S(1)}, u32[]{:S(2)}, u32[]{:S(2)}) collective-permute-start(bf16[512,384]{1,0:T(8,128)(2,1)S(1)} %get-tuple-element.242), channel_id=1, source_target_pairs={{0,24},{4,28},{8,16},{12,20},{16,8},{20,12},{24,0},{28,4},{1,25},{... | collective-permute-start | bytes 1179656 | tf_op jit(solution)/shard_map/ppermute | solution.py:1164
  376.2 16.7 %collective-permute-start.44 = (bf16[256,2048]{1,0:T(8,128)(2,1)}, bf16[256,2048]{1,0:T(8,128)(2,1)}, u32[]{:S(2)}, u32[]{:S(2)}) collective-permute-start(bf16[256,2048]{1,0:T(8,128)(2,1)} %get-tuple-element.246.refs_2_), channel_id=1, source_target_pairs={{0,1},{1,0},{2,3},{3,2},{4,5},{5,4},{6,7},{7,6},{8,9},{9,8},{10,11... | collective-permute-start | bytes 3145736 | tf_op jit(solution)/shard_map/ppermute | solution.py:1167
  376.3 34.2 %collective-permute-start.49 = (bf16[3,128,2048]{2,1,0:T(8,128)(2,1)S(1)}, bf16[3,128,2048]{2,1,0:T(8,128)(2,1)}, u32[]{:S(2)}, u32[]{:S(2)}) collective-permute-start(bf16[3,128,2048]{2,1,0:T(8,128)(2,1)S(1)} %stack_rows.1.refs_5_.refs_3_), channel_id=1, source_target_pairs={{0,1},{1,0},{2,3},{3,2},{4,5},{5,4},{6,7},{7,6},{8,9},{9,8},{10,11... | collective-permute-start | bytes 4718600 | tf_op jit(solution)/shard_map/ppermute | solution.py:1167
  376.8 36.0 %collective-permute-start.50 = (bf16[3,128,2048]{2,1,0:T(8,128)(2,1)}, bf16[3,128,2048]{2,1,0:T(8,128)(2,1)}, u32[]{:S(2)}, u32[]{:S(2)}) collective-permute-start(bf16[3,128,2048]{2,1,0:T(8,128)(2,1)} %collective-permute-done.37.refs_5_), channel_id=1, source_target_pairs={{0,1},{1,0},{2,3},{3,2},{4,5},{5,4},{6,7},{7,6},{8,9},{9,8},{10,11... | collective-permute-start | bytes 4718600 | tf_op jit(solution)/shard_map/ppermute | solution.py:1167
  376.9 75.2 %collective-permute-start.57 = (bf16[512,1024]{1,0:T(8,128)(2,1)}, bf16[512,1024]{1,0:T(8,128)(2,1)}, u32[]{:S(2)}, u32[]{:S(2)}) collective-permute-start(bf16[512,1024]{1,0:T(8,128)(2,1)} %get-tuple-element.273), channel_id=1, source_target_pairs={{0,16},{4,20},{8,24},{12,28},{16,0},{20,4},{24,8},{28,12},{1,17},{... | collective-permute-start | bytes 3145736 | tf_op jit(solution)/shard_map/ppermute | solution.py:1164
  384.0 40.3 %collective-permute-start.51 = (bf16[256,1024]{1,0:T(8,128)(2,1)}, bf16[256,1024]{1,0:T(8,128)(2,1)}, u32[]{:S(2)}, u32[]{:S(2)}) collective-permute-start(bf16[256,1024]{1,0:T(8,128)(2,1)} %get-tuple-element.262), channel_id=1, source_target_pairs={{0,8},{4,12},{8,0},{12,4},{16,24},{20,28},{24,16},{28,20},{1,9},{5... | collective-permute-start | bytes 1572872 | tf_op jit(solution)/shard_map/ppermute | solution.py:1164
  407.7 31.0 %collective-permute-start.48 = (bf16[1024,512]{1,0:T(8,128)(2,1)}, bf16[1024,512]{1,0:T(8,128)(2,1)}, u32[]{:S(2)}, u32[]{:S(2)}) collective-permute-start(bf16[1024,512]{1,0:T(8,128)(2,1)} %get-tuple-element.258.refs_2_), channel_id=1, source_target_pairs={{0,4},{4,0},{8,12},{12,8},{16,20},{20,16},{24,28},{28,24},{1,5},{5... | collective-permute-start | bytes 3145736 | tf_op jit(solution)/shard_map/ppermute | solution.py:1164
  410.5 63.8 %collective-permute-start.53 = (bf16[512,1024]{1,0:T(8,128)(2,1)}, bf16[512,1024]{1,0:T(8,128)(2,1)S(1)}, u32[]{:S(2)}, u32[]{:S(2)}) collective-permute-start(bf16[512,1024]{1,0:T(8,128)(2,1)} %get-tuple-element.269), channel_id=1, source_target_pairs={{0,16},{4,20},{8,24},{12,28},{16,0},{20,4},{24,8},{28,12},{1,17},{... | collective-permute-start | bytes 3145736 | tf_op jit(solution)/shard_map/ppermute | solution.py:1164
  412.8 28.1 %collective-permute-start.46 = (bf16[128,2048]{1,0:T(8,128)(2,1)S(1)}, bf16[128,2048]{1,0:T(8,128)(2,1)S(1)}, u32[]{:S(2)}, u32[]{:S(2)}) collective-permute-start(bf16[128,2048]{1,0:T(8,128)(2,1)S(1)} %get-tuple-element.255.refs_0_), channel_id=1, source_target_pairs={{0,2},{1,3},{2,0},{3,1},{4,6},{5,7},{6,4},{7,5},{8,10},{9,11},{10,... | collective-permute-start | bytes 1572872 | tf_op jit(solution)/shard_map/ppermute | solution.py:1167
  442.1 54.1 %collective-permute-start.52 = (bf16[256,2048]{1,0:T(8,128)(2,1)S(1)}, bf16[256,2048]{1,0:T(8,128)(2,1)S(1)}, u32[]{:S(2)}, u32[]{:S(2)}) collective-permute-start(bf16[256,2048]{1,0:T(8,128)(2,1)S(1)} %copy-done.95), channel_id=1, source_target_pairs={{0,8},{4,12},{8,0},{12,4},{16,24},{20,28},{24,16},{28,20},{1,9},{5... | collective-permute-start | bytes 3145736 | tf_op jit(solution)/shard_map/ppermute | solution.py:1164
  442.8 16.6 %collective-permute-start.54 = (bf16[1024,384]{1,0:T(8,128)(2,1)S(1)}, bf16[1024,384]{1,0:T(8,128)(2,1)S(1)}, u32[]{:S(2)}, u32[]{:S(2)}) collective-permute-start(bf16[1024,384]{1,0:T(8,128)(2,1)S(1)} %get-tuple-element.272.refs_2_), channel_id=1, source_target_pairs={{0,4},{4,0},{8,12},{12,8},{16,20},{20,16},{24,28},{28,24},{1,5},{5... | collective-permute-start | bytes 2359304 | tf_op jit(solution)/shard_map/ppermute | solution.py:1164
  496.5 24.7 %collective-permute-start.59 = (bf16[256,2048]{1,0:T(8,128)(2,1)S(1)}, bf16[256,2048]{1,0:T(8,128)(2,1)S(1)}, u32[]{:S(2)}, u32[]{:S(2)}) collective-permute-start(bf16[256,2048]{1,0:T(8,128)(2,1)S(1)} %row_sum.9.refs_0_.refs_2_), channel_id=1, source_target_pairs={{0,2},{1,3},{2,0},{3,1},{4,6},{5,7},{6,4},{7,5},{8,10},{9,11},{10,... | collective-permute-start | bytes 3145736 | tf_op jit(solution)/shard_map/ppermute | solution.py:1167
  497.1 24.5 %collective-permute-start.65 = (bf16[512,512]{1,0:T(8,128)(2,1)S(1)}, bf16[512,512]{1,0:T(8,128)(2,1)S(1)}, u32[]{:S(2)}, u32[]{:S(2)}) collective-permute-start(bf16[512,512]{1,0:T(8,128)(2,1)S(1)} %get-tuple-element.293), channel_id=1, source_target_pairs={{0,16},{4,20},{8,24},{12,28},{16,0},{20,4},{24,8},{28,12},{1,17},{... | collective-permute-start | bytes 1572872 | tf_op jit(solution)/shard_map/ppermute | solution.py:1164
  497.6 27.0 %collective-permute-start.64 = (bf16[256,1024]{1,0:T(8,128)(2,1)}, bf16[256,1024]{1,0:T(8,128)(2,1)}, u32[]{:S(2)}, u32[]{:S(2)}) collective-permute-start(bf16[256,1024]{1,0:T(8,128)(2,1)} %get-tuple-element.292), channel_id=1, source_target_pairs={{0,8},{4,12},{8,0},{12,4},{16,24},{20,28},{24,16},{28,20},{1,9},{5... | collective-permute-start | bytes 1572872 | tf_op jit(solution)/shard_map/ppermute | solution.py:1164
  501.4 40.6 %collective-permute-start.63 = (bf16[256,1024]{1,0:T(8,128)(2,1)}, bf16[256,1024]{1,0:T(8,128)(2,1)}, u32[]{:S(2)}, u32[]{:S(2)}) collective-permute-start(bf16[256,1024]{1,0:T(8,128)(2,1)} %get-tuple-element.291), channel_id=1, source_target_pairs={{0,8},{4,12},{8,0},{12,4},{16,24},{20,28},{24,16},{28,20},{1,9},{5... | collective-permute-start | bytes 1572872 | tf_op jit(solution)/shard_map/ppermute | solution.py:1164
  521.4 31.7 %collective-permute-start.60 = (bf16[256,2048]{1,0:T(8,128)(2,1)S(1)}, bf16[256,2048]{1,0:T(8,128)(2,1)}, u32[]{:S(2)}, u32[]{:S(2)}) collective-permute-start(bf16[256,2048]{1,0:T(8,128)(2,1)S(1)} %add_rows.1.refs_1_), channel_id=1, source_target_pairs={{0,1},{1,0},{2,3},{3,2},{4,5},{5,4},{6,7},{7,6},{8,9},{9,8},{10,11... | collective-permute-start | bytes 3145736 | tf_op jit(solution)/shard_map/ppermute | solution.py:1167
  523.2 25.4 %collective-permute-start.69 = (bf16[256,512]{1,0:T(8,128)(2,1)}, bf16[256,512]{1,0:T(8,128)(2,1)S(1)}, u32[]{:S(2)}, u32[]{:S(2)}) collective-permute-start(bf16[256,512]{1,0:T(8,128)(2,1)} %get-tuple-element.303), channel_id=1, source_target_pairs={{0,8},{4,12},{8,0},{12,4},{16,24},{20,28},{24,16},{28,20},{1,9},{5... | collective-permute-start | bytes 786440 | tf_op jit(solution)/shard_map/ppermute | solution.py:1164
  524.7 32.9 %collective-permute-start.66 = (bf16[256,384]{1,0:T(8,128)(2,1)}, bf16[256,384]{1,0:T(8,128)(2,1)}, u32[]{:S(2)}, u32[]{:S(2)}) collective-permute-start(bf16[256,384]{1,0:T(8,128)(2,1)} %copy-done.76), channel_id=1, source_target_pairs={{0,8},{4,12},{8,0},{12,4},{16,24},{20,28},{24,16},{28,20},{1,9},{5... | collective-permute-start | bytes 589832 | tf_op jit(solution)/shard_map/ppermute | solution.py:1164
  537.9 19.7 %collective-permute-start.67 = (bf16[256,384]{1,0:T(8,128)(2,1)}, bf16[256,384]{1,0:T(8,128)(2,1)}, u32[]{:S(2)}, u32[]{:S(2)}) collective-permute-start(bf16[256,384]{1,0:T(8,128)(2,1)} %get-tuple-element.298), channel_id=1, source_target_pairs={{0,16},{4,20},{8,24},{12,28},{16,0},{20,4},{24,8},{28,12},{1,17},{... | collective-permute-start | bytes 589832 | tf_op jit(solution)/shard_map/ppermute | solution.py:1164
  (121 other events, 1440.4 us)
